TPU v7x, 512 devices: a whole 4x4x16 slice. The times are simulated.
512 devices in a mesh: dp: 32 (over z_hi, y, core), seq: 16 (over z_lo, x).
Axes of the slice: x: 4, y: 4, z: 16 (z_hi: 4, z_lo: 4; z = z_hi * 4 + z_lo), core: 2. Of those that a mesh axis runs over, the one named last changes fastest.
Arguments:
- cond_vec: float32 [32, 3072], P('dp', 'seq'), may hold values from -6 to 6
- mod_weight: bfloat16 [2, 3072, 3072], P(None, 'seq', 'dp'), may hold values from -0.109375 to 0.109375
- text_hidden: bfloat16 [32, 512, 3072], P('dp', 'seq'), may hold values from -121 to 121
- text_grad: bfloat16 [32, 512, 3072], P('dp', 'seq'), may hold values from -14 to 14, as said below
- queries: bfloat16 [32, 2048, 2048], P('dp', 'seq'), may hold values from -4.5 to 4.5
- keys: bfloat16 [32, 2048, 2048], P('dp', 'seq'), may hold values from -4.5 to 4.5
- values: bfloat16 [32, 2048, 2048], P('dp', 'seq'), may hold values from -6 to 6
- out_grad: bfloat16 [32, 2048, 2048], P('dp', 'seq'), may hold values from -6 to 6
Outputs:
- text_hidden_grad: bfloat16 [32, 512, 3072], P('dp', 'seq')
- mod_weight_grad: float32 [2, 3072, 3072], P(None, 'seq', 'dp')
- cond_vec_grad: float32 [32, 3072], P('dp', 'seq')
- query_grad: bfloat16 [32, 2048, 2048], P('dp', 'seq')
- key_grad: bfloat16 [32, 2048, 2048], P('dp', 'seq')
- value_grad: bfloat16 [32, 2048, 2048], P('dp', 'seq')
Inputs may be any that keep to these rules, and one draw needn't show every extreme that they name: `text_grad`: incoming gradient.
All inputs are finite; a program needn't handle non-finite values.
Results may differ from a plain program's by a relative error of at most 0.0087.
Values may be sent and summed in bfloat16 or wider, within the bound.
A program may use at most 64 MiB of HBM per device.

v0:
```python
import math

import jax
import jax.numpy as jnp
from jax import lax
from jax.sharding import Mesh
from jax.sharding import PartitionSpec as P

HEADS = 16
HEAD_DIM = 128
DP = ("dp_0", "dp_1", "dp_2")


norm_eps = 1e-06


def from_everyone(x, axis):
    copies = jnp.broadcast_to(x, (lax.axis_size(axis), *x.shape))
    return lax.all_to_all(copies, axis, split_axis=0, concat_axis=0, tiled=True)


def joined_along(tiles, dim):
    tiles = jnp.moveaxis(tiles, 0, dim)
    shape = tiles.shape
    return tiles.reshape(*shape[:dim], shape[dim] * shape[dim + 1], *shape[dim + 2 :])


def collect(x, axis, dim):
    tiles = from_everyone(x, axis)
    return joined_along(tiles, dim)


def taken_together(x, axis):
    everything = from_everyone(x, axis)
    return jnp.sum(everything, axis=0)


def grouped_exchange(x, axis, split_dim, concat_dim, work, item_dim, out_dim):
    items = jax.tree.leaves(x)[0].shape[item_dim]
    count = 2 if items % 2 == 0 else 1
    finished = []
    for k in range(count):
        group = jax.tree.map(
            lambda a: lax.slice_in_dim(
                a, k * (items // count), (k + 1) * (items // count), axis=item_dim
            ),
            x,
        )
        finished.append(
            work(
                lax.all_to_all(
                    group, axis, split_axis=split_dim, concat_axis=concat_dim, tiled=True
                )
            )
        )
    return jax.tree.map(lambda *parts: jnp.concatenate(parts, axis=out_dim), *finished)


def sent_together(arrays, axis, split_dim, concat_dim, along):
    both = jnp.concatenate(arrays, axis=along)
    whole, at, finished = (
        lax.all_to_all(both, axis, split_axis=split_dim, concat_axis=concat_dim, tiled=True),
        0,
        [],
    )
    for a in arrays:
        finished.append(lax.slice_in_dim(whole, at, at + a.shape[along], axis=along))
        at += a.shape[along]
    return tuple(finished)


def split_up(x, dim, devices):
    shape = x.shape
    tiles = x.reshape(*shape[:dim], devices, shape[dim] // devices, *shape[dim + 1 :])
    return jnp.moveaxis(tiles, dim, 0)


def moved_by_axis(tiles, axes, sequence):
    shape = [lax.axis_size(a) for a in axes]
    tiles = tiles.reshape(*shape, *tiles.shape[1:])
    for k in sequence:
        tiles = lax.all_to_all(tiles, axes[k], split_axis=k, concat_axis=k, tiled=True)
    return tiles.reshape(-1, *tiles.shape[len(axes) :])


def exchange_by_chip(x, groups, sequence, split_dim, concat_dim):
    devices = lax.axis_size(groups[0]) * lax.axis_size(groups[1])
    tiles = split_up(x, split_dim, devices)
    return joined_along(moved_by_axis(tiles, groups, sequence), concat_dim)


def summed_on_arrival(x, axis, dim):
    tiles = split_up(x, dim, lax.axis_size(axis))
    arrived = lax.all_to_all(tiles, axis, split_axis=0, concat_axis=0, tiled=True)
    return arrived.sum(axis=0)


def attend_items(query, key_rows, value, grad_out):
    items, rows, width = query.shape
    factor = width ** (-0.5)
    block = math.gcd(rows, 512)
    count = rows // block

    def split_rows(array):
        return array.reshape(items, count, block, width).transpose(1, 0, 2, 3)

    def one_block(carry, pieces):
        key_total, value_total = carry
        query_part, grad_part = pieces
        scores = (
            jnp.einsum("isd,itd->ist", query_part, key_rows, preferred_element_type=jnp.float32)
            * factor
        )
        peak = jnp.max(scores, axis=-1, keepdims=True)
        exponent = jnp.exp(scores - peak)
        probability = exponent / jnp.sum(exponent, axis=-1, keepdims=True)
        prob_low = probability.astype(jnp.bfloat16)
        attn_out = jnp.einsum("ist,itd->isd", prob_low, value, preferred_element_type=jnp.float32)
        row_delta = jnp.sum(grad_part.astype(jnp.float32) * attn_out, axis=-1, keepdims=True)
        value_total = value_total + jnp.einsum(
            "ist,isd->itd", prob_low, grad_part, preferred_element_type=jnp.float32
        )
        prob_grad = jnp.einsum("isd,itd->ist", grad_part, value, preferred_element_type=jnp.float32)
        score_low = (probability * (prob_grad - row_delta) * factor).astype(jnp.bfloat16)
        query_part_grad = jnp.einsum(
            "ist,itd->isd", score_low, key_rows, preferred_element_type=jnp.float32
        ).astype(jnp.bfloat16)
        key_total = key_total + jnp.einsum(
            "ist,isd->itd", score_low, query_part, preferred_element_type=jnp.float32
        )
        return ((key_total, value_total), query_part_grad)

    empty = jnp.zeros((items, rows, width), jnp.float32)
    totals, query_blocks = lax.scan(
        one_block, (empty, empty), (split_rows(query), split_rows(grad_out))
    )
    query_grad = query_blocks.transpose(1, 0, 2, 3).reshape(items, rows, width)
    return (query_grad, totals[0].astype(jnp.bfloat16), totals[1].astype(jnp.bfloat16))


def attend_local(pieces):
    grads = attend_items(pieces[0][0], pieces[1][0], pieces[2][0], pieces[3][0])
    return (grads[0][None], grads[1][None], grads[2][None])


def into_pairs(array):
    samples, local_rows, features = array.shape
    ordered = array.reshape(samples, local_rows, HEADS, HEAD_DIM).transpose(2, 0, 1, 3)
    return ordered


def from_pairs(array, samples):
    local_rows = array.shape[2]
    shaped = array.transpose(1, 2, 0, 3)
    return shaped.reshape(samples, local_rows, HEADS * HEAD_DIM)


def per_device(cond_vec, mod_weight, text_hidden, text_grad, queries, keys, values, out_grad):
    samples = queries.shape[0]
    cond_all = collect(cond_vec, DP, 0)
    act = jax.nn.silu(cond_all).astype(jnp.bfloat16)
    partial_scale = jnp.dot(act, mod_weight[1], preferred_element_type=jnp.float32)
    summed_scale = taken_together(partial_scale, "seq")
    mod_scale = lax.all_to_all(summed_scale, DP, split_axis=0, concat_axis=1, tiled=True)
    hidden = text_hidden.astype(jnp.float32)
    incoming = text_grad.astype(jnp.float32)
    centred = hidden - jnp.mean(hidden, axis=-1, keepdims=True)
    inv_std = lax.rsqrt(jnp.mean(centred * centred, axis=-1, keepdims=True) + norm_eps)
    normed = centred * inv_std
    grad_mod = jnp.stack([jnp.sum(incoming, axis=1), jnp.sum(incoming * normed, axis=1)], axis=1)
    upstream = incoming * (1.0 + mod_scale[:, None, :])
    text_hidden_grad = inv_std * (
        upstream
        - jnp.mean(upstream, axis=-1, keepdims=True)
        - normed * jnp.mean(upstream * normed, axis=-1, keepdims=True)
    )
    text_hidden_grad = text_hidden_grad.astype(jnp.bfloat16)
    pairs = (into_pairs(queries), into_pairs(keys), into_pairs(values), into_pairs(out_grad))
    query_pairs, key_pairs, value_pairs = grouped_exchange(
        (pairs[0], pairs[1], pairs[2], pairs[3]), "seq", 0, 2, attend_local, 1, 1
    )
    query_pairs, key_pairs, value_pairs = sent_together(
        (query_pairs, key_pairs, value_pairs), "seq", 2, 0, 1
    )
    summed_grad = taken_together(grad_mod, "seq")
    owner_grad = exchange_by_chip(summed_grad, (("dp_0", "dp_1"), "dp_2"), (1, 0), 2, 0)
    mod_weight_grad = jnp.einsum(
        "br,bkc->krc", act.astype(jnp.float32), owner_grad, precision=lax.Precision.HIGHEST
    )
    backward = jnp.einsum(
        "bkc,krc->br", owner_grad, mod_weight.astype(jnp.float32), precision=lax.Precision.HIGHEST
    )
    summed_back = summed_on_arrival(backward, DP, 0)
    sigma = jax.nn.sigmoid(cond_vec)
    cond_vec_grad = summed_back * sigma * (1.0 + cond_vec * (1.0 - sigma))
    query_grad = from_pairs(query_pairs, samples)
    key_grad = from_pairs(key_pairs, samples)
    value_grad = from_pairs(value_pairs, samples)
    return (text_hidden_grad, mod_weight_grad, cond_vec_grad, query_grad, key_grad, value_grad)


def solution(mesh):
    finer = Mesh(mesh.devices.reshape(4, 4, 2, mesh.shape["seq"]), ("dp_0", "dp_1", "dp_2", "seq"))
    placed = (
        P(DP, "seq"),
        P(None, "seq", DP),
        P(DP, "seq", None),
        P(DP, "seq", None),
        P(DP, "seq", None),
        P(DP, "seq", None),
        P(DP, "seq", None),
        P(DP, "seq", None),
    )
    return jax.shard_map(
        per_device,
        mesh=finer,
        in_specs=placed,
        out_specs=(
            P(DP, "seq", None),
            P(None, "seq", DP),
            P(DP, "seq"),
            P(DP, "seq", None),
            P(DP, "seq", None),
            P(DP, "seq", None),
        ),
        check_vma=False,
    )
```

profile of v0, /device:TPU:64, one launch (start us, length us, event | category | flops | bytes accessed | tf_op | source)
XLA Modules:
  0.0 329.1 jit_solution(1264877118851377033)
XLA Ops:
  1.4 30.8 %all_to_all.97 = f32[32,1,192]{2,1,0:T(1,128)S(1)} all-to-all(f32[32,1,192]{2,1,0:T(1,128)S(1)} %broadcast_in_dim.33), channel_id=1, replica_groups=mesh['dp_0'=4,'dp_1'=4,'dp_2'=2,'seq'=16] {'dp_0','dp_1','dp_2'}, dimensions={0} | all-to-all | bytes 49152 | tf_op jit(solution)/shard_map/all_to_all | solution.py:19
  33.2 16.1 %all_to_all.98 = f32[16,32,96]{2,1,0:T(8,128)S(1)} all-to-all(f32[16,32,96]{2,1,0:T(8,128)S(1)} %broadcast_in_dim.34), channel_id=1, replica_groups=mesh['dp_0'=4,'dp_1'=4,'dp_2'=2,'seq'=16] {'seq'}, dimensions={0} | all-to-all | bytes 393216 | tf_op jit(solution)/shard_map/all_to_all | solution.py:19
  49.9 3.8 %all-to-all-start.2 = ((f32[32,1,96]{2,1,0:T(1,128)}), f32[32,1,96]{2,1,0:T(1,128)S(1)}, u32[]{:S(2)}, u32[]{:S(2)}) async-start(f32[32,1,96]{2,1,0:T(1,128)} %bitcast.4), calls=%async_computation.2 | async-start | bytes 32768 | tf_op jit(solution)/shard_map/all_to_all | solution.py:164
  56.1 12.2 %all-to-all-done.2 = f32[32,1,96]{2,1,0:T(1,128)S(1)} async-done(((f32[32,1,96]{2,1,0:T(1,128)}), f32[32,1,96]{2,1,0:T(1,128)S(1)}, u32[]{:S(2)}, u32[]{:S(2)}) %all-to-all-start.2) | async-done | bytes 12320 | tf_op jit(solution)/shard_map/all_to_all | solution.py:164
  68.3 5.9 %all-to-all-start.7 = ((bf16[16,1,128,128]{3,2,1,0:T(8,128)(2,1)}), bf16[16,1,128,128]{3,2,1,0:T(8,128)(2,1)}, u32[]{:S(2)}, u32[]{:S(2)}) async-start(bf16[16,1,128,128]{3,2,1,0:T(8,128)(2,1)} %copy.99), calls=%async_computation.7 | async-start | bytes 1048576 | tf_op jit(solution)/shard_map/all_to_all | solution.py:51
  75.5 13.6 %all-to-all-done.7 = bf16[16,1,128,128]{3,2,1,0:T(8,128)(2,1)} async-done(((bf16[16,1,128,128]{3,2,1,0:T(8,128)(2,1)}), bf16[16,1,128,128]{3,2,1,0:T(8,128)(2,1)}, u32[]{:S(2)}, u32[]{:S(2)}) %all-to-all-start.7) | async-done | bytes 524320 | tf_op jit(solution)/shard_map/all_to_all | solution.py:51
  89.1 5.4 %all-to-all-start.8 = ((bf16[16,1,128,128]{3,2,1,0:T(8,128)(2,1)}), bf16[16,1,128,128]{3,2,1,0:T(8,128)(2,1)S(1)}, u32[]{:S(2)}, u32[]{:S(2)}) async-start(bf16[16,1,128,128]{3,2,1,0:T(8,128)(2,1)} %copy.101), calls=%async_computation.8 | async-start | bytes 1048576 | tf_op jit(solution)/shard_map/all_to_all | solution.py:51
  95.4 12.8 %all-to-all-done.8 = bf16[16,1,128,128]{3,2,1,0:T(8,128)(2,1)S(1)} async-done(((bf16[16,1,128,128]{3,2,1,0:T(8,128)(2,1)}), bf16[16,1,128,128]{3,2,1,0:T(8,128)(2,1)S(1)}, u32[]{:S(2)}, u32[]{:S(2)}) %all-to-all-start.8) | async-done | bytes 524320 | tf_op jit(solution)/shard_map/all_to_all | solution.py:51
  108.2 5.4 %all-to-all-start.9 = ((bf16[16,1,128,128]{2,3,1,0:T(8,128)(2,1)}), bf16[16,1,128,128]{2,3,1,0:T(8,128)(2,1)S(1)}, u32[]{:S(2)}, u32[]{:S(2)}) async-start(bf16[16,1,128,128]{2,3,1,0:T(8,128)(2,1)} %bitcast.25), calls=%async_computation.9 | async-start | bytes 1048576 | tf_op jit(solution)/shard_map/all_to_all | solution.py:51
  115.9 11.0 %all-to-all-done.9 = bf16[16,1,128,128]{2,3,1,0:T(8,128)(2,1)S(1)} async-done(((bf16[16,1,128,128]{2,3,1,0:T(8,128)(2,1)}), bf16[16,1,128,128]{2,3,1,0:T(8,128)(2,1)S(1)}, u32[]{:S(2)}, u32[]{:S(2)}) %all-to-all-start.9) | async-done | bytes 524320 | tf_op jit(solution)/shard_map/all_to_all | solution.py:51
  126.9 5.4 %all-to-all-start.10 = ((bf16[16,1,128,128]{3,2,1,0:T(8,128)(2,1)}), bf16[16,1,128,128]{3,2,1,0:T(8,128)(2,1)S(1)}, u32[]{:S(2)}, u32[]{:S(2)}) async-start(bf16[16,1,128,128]{3,2,1,0:T(8,128)(2,1)} %copy.106), calls=%async_computation.10 | async-start | bytes 1048576 | tf_op jit(solution)/shard_map/all_to_all | solution.py:51
  133.5 11.9 %all-to-all-done.10 = bf16[16,1,128,128]{3,2,1,0:T(8,128)(2,1)S(1)} async-done(((bf16[16,1,128,128]{3,2,1,0:T(8,128)(2,1)}), bf16[16,1,128,128]{3,2,1,0:T(8,128)(2,1)S(1)}, u32[]{:S(2)}, u32[]{:S(2)}) %all-to-all-start.10) | async-done | bytes 524320 | tf_op jit(solution)/shard_map/all_to_all | solution.py:51
  146.2 5.4 %all-to-all-start.3 = ((f32[16,1,2,3072]{3,2,1,0:T(2,128)}), f32[16,1,2,3072]{3,2,1,0:T(2,128)}, u32[]{:S(2)}, u32[]{:S(2)}) async-start(f32[16,1,2,3072]{3,2,1,0:T(2,128)} %broadcast_in_dim.35), calls=%async_computation.3 | async-start | bytes 786432 | tf_op jit(solution)/shard_map/all_to_all | solution.py:19
  151.5 67.7 %while.15 = (s32[]{:T(128)}, f32[1,2048,128]{2,1,0:T(8,128)}, f32[1,2048,128]{2,1,0:T(8,128)}, bf16[4,1,512,128]{3,2,1,0:T(8,128)(2,1)}, bf16[4,1,512,128]{3,2,1...) while((s32[]{:T(128)}, f32[1,2048,128]{2,1,0:T(8,128)}, ...), condition=%wide.region_13.14_spmd.clone, body=%wide.region_9.13_spmd.clone.sunk | while | flops 1626601984 | bytes 81018592 | solution.py:134
  151.5 1.8 multiply_reduce_fusion.2
  154.2 2.7 fusion.71
  157.1 3.2 fusion.72
  161.3 2.8 fusion.73
  164.1 1.4 fusion.75
  165.4 1.8 fusion.74
  167.2 1.8 multiply_reduce_fusion.2
  169.9 2.7 fusion.71
  172.8 3.2 fusion.72
  177.0 3.2 fusion.73
  180.1 1.4 fusion.75
  181.5 3.1 fusion.74
  184.6 1.8 multiply_reduce_fusion.2
  187.2 2.7 fusion.71
  190.1 3.2 fusion.72
  194.3 3.2 fusion.73
  197.5 1.4 fusion.75
  198.8 3.1 fusion.74
  201.9 1.8 multiply_reduce_fusion.2
  204.5 2.7 fusion.71
  207.4 3.2 fusion.72
  211.6 3.2 fusion.73
  216.2 3.1 fusion.74
  220.5 3.7 %all_to_all.99 = f32[16,2,1,2,96]{4,0,3,2,1:T(8,128)S(1)} all-to-all(f32[16,2,1,2,96]{4,0,3,2,1:T(8,128)S(1)} %copy.94), channel_id=1, replica_groups=mesh['dp_0'=4,'dp_1'=4,'dp_2'=2,'seq'=16] {'dp_2'}, dimensions={1} | all-to-all | bytes 49152 | tf_op jit(solution)/shard_map/all_to_all | solution.py:82
  224.9 3.5 %all-to-all-start.5 = ((f32[16,2,1,2,96]{4,1,3,2,0:T(2,128)}), f32[16,2,1,2,96]{4,1,3,2,0:T(2,128)S(1)}, u32[]{:S(2)}, u32[]{:S(2)}) async-start(f32[16,2,1,2,96]{4,1,3,2,0:T(2,128)} %copy.95), calls=%async_computation.5 | async-start | bytes 65536 | tf_op jit(solution)/shard_map/all_to_all | solution.py:82
  228.4 1.7 convert_bitcast_fusion
  230.1 13.1 %all-to-all-done.5 = f32[16,2,1,2,96]{4,1,3,2,0:T(2,128)S(1)} async-done(((f32[16,2,1,2,96]{4,1,3,2,0:T(2,128)}), f32[16,2,1,2,96]{4,1,3,2,0:T(2,128)S(1)}, u32[]{:S(2)}, u32[]{:S(2)}) %all-to-all-start.5) | async-done | bytes 24608 | tf_op jit(solution)/shard_map/all_to_all | solution.py:82
  245.0 4.0 %all-to-all-start.6 = ((f32[32,1,192]{2,1,0:T(1,128)}), f32[32,1,192]{2,1,0:T(1,128)S(1)}, u32[]{:S(2)}, u32[]{:S(2)}) async-start(f32[32,1,192]{2,1,0:T(1,128)} %copy.97), calls=%async_computation.6 | async-start | bytes 65536 | tf_op jit(solution)/shard_map/all_to_all | solution.py:94
  249.3 10.8 %copy.109 = bf16[1,3,2048,128]{3,1,0,2:T(4,128)(2,1)} copy(bf16[1,3,2048,128]{3,2,1,0:T(8,128)(2,1)S(1)} %pad_maximum_fusion) | data formatting | bytes 3145728 | tf_op jit(solution)/shard_map/concatenate | solution.py:60
  260.1 3.7 %all-to-all-done.6 = f32[32,1,192]{2,1,0:T(1,128)S(1)} async-done(((f32[32,1,192]{2,1,0:T(1,128)}), f32[32,1,192]{2,1,0:T(1,128)S(1)}, u32[]{:S(2)}, u32[]{:S(2)}) %all-to-all-start.6) | async-done | bytes 24608 | tf_op jit(solution)/shard_map/all_to_all | solution.py:94
  263.8 7.4 %all-to-all-start.11 = ((bf16[1,3,2048,128]{3,1,0,2:T(4,128)(2,1)}), bf16[1,3,2048,128]{3,1,0,2:T(4,128)(2,1)S(1)}, u32[]{:S(2)}, u32[]{:S(2)}) async-start(bf16[1,3,2048,128]{3,1,0,2:T(4,128)(2,1)} %copy.109), calls=%async_computation.11 | async-start | bytes 4194304 | tf_op jit(solution)/shard_map/all_to_all | solution.py:62
  273.8 45.9 %all-to-all-done.11 = bf16[1,3,2048,128]{3,1,0,2:T(4,128)(2,1)S(1)} async-done(((bf16[1,3,2048,128]{3,1,0,2:T(4,128)(2,1)}), bf16[1,3,2048,128]{3,1,0,2:T(4,128)(2,1)S(1)}, u32[]{:S(2)}, u32[]{:S(2)}) %all-to-all-start.11) | async-done | bytes 1572896 | tf_op jit(solution)/shard_map/all_to_all | solution.py:62
  319.7 3.3 slice_bitcast_fusion
  324.6 1.8 copy.111
  (107 shorter events, 31.2 us)
Async XLA Ops:
  0.6 73.5 %copy-start.7 = (bf16[1,128,2048]{2,1,0:T(8,128)(2,1)S(1)}, bf16[1,128,2048]{2,1,0:T(8,128)(2,1)}, u32[]{:S(2)}) copy-start(bf16[1,128,2048]{2,1,0:T(8,128)(2,1)} %param.15) | copy-start | bytes 1572868
  0.6 93.8 %copy-start.8 = (bf16[1,128,2048]{2,1,0:T(8,128)(2,1)S(1)}, bf16[1,128,2048]{2,1,0:T(8,128)(2,1)}, u32[]{:S(2)}) copy-start(bf16[1,128,2048]{2,1,0:T(8,128)(2,1)} %param.17) | copy-start | bytes 1572868
  49.9 18.4 %all-to-all-start.2 = ((f32[32,1,96]{2,1,0:T(1,128)}), f32[32,1,96]{2,1,0:T(1,128)S(1)}, u32[]{:S(2)}, u32[]{:S(2)}) async-start(f32[32,1,96]{2,1,0:T(1,128)} %bitcast.4), calls=%async_computation.2 | async-start | bytes 32768 | tf_op jit(solution)/shard_map/all_to_all | solution.py:164
  68.3 20.8 %all-to-all-start.7 = ((bf16[16,1,128,128]{3,2,1,0:T(8,128)(2,1)}), bf16[16,1,128,128]{3,2,1,0:T(8,128)(2,1)}, u32[]{:S(2)}, u32[]{:S(2)}) async-start(bf16[16,1,128,128]{3,2,1,0:T(8,128)(2,1)} %copy.99), calls=%async_computation.7 | async-start | bytes 1048576 | tf_op jit(solution)/shard_map/all_to_all | solution.py:51
  74.1 58.2 %copy-start.2 = (bf16[1,32,3072]{2,1,0:T(8,128)(2,1)S(1)}, bf16[1,32,3072]{2,1,0:T(8,128)(2,1)}, u32[]{:S(2)}) copy-start(bf16[1,32,3072]{2,1,0:T(8,128)(2,1)} %param.12) | copy-start | bytes 589828
  74.2 58.7 %copy-start.5 = (bf16[1,32,3072]{2,1,0:T(8,128)(2,1)S(1)}, bf16[1,32,3072]{2,1,0:T(8,128)(2,1)}, u32[]{:S(2)}) copy-start(bf16[1,32,3072]{2,1,0:T(8,128)(2,1)} %param.13) | copy-start | bytes 589828
  89.1 19.1 %all-to-all-start.8 = ((bf16[16,1,128,128]{3,2,1,0:T(8,128)(2,1)}), bf16[16,1,128,128]{3,2,1,0:T(8,128)(2,1)S(1)}, u32[]{:S(2)}, u32[]{:S(2)}) async-start(bf16[16,1,128,128]{3,2,1,0:T(8,128)(2,1)} %copy.101), calls=%async_computation.8 | async-start | bytes 1048576 | tf_op jit(solution)/shard_map/all_to_all | solution.py:51
  108.2 18.7 %all-to-all-start.9 = ((bf16[16,1,128,128]{2,3,1,0:T(8,128)(2,1)}), bf16[16,1,128,128]{2,3,1,0:T(8,128)(2,1)S(1)}, u32[]{:S(2)}, u32[]{:S(2)}) async-start(bf16[16,1,128,128]{2,3,1,0:T(8,128)(2,1)} %bitcast.25), calls=%async_computation.9 | async-start | bytes 1048576 | tf_op jit(solution)/shard_map/all_to_all | solution.py:51
  126.9 18.4 %all-to-all-start.10 = ((bf16[16,1,128,128]{3,2,1,0:T(8,128)(2,1)}), bf16[16,1,128,128]{3,2,1,0:T(8,128)(2,1)S(1)}, u32[]{:S(2)}, u32[]{:S(2)}) async-start(bf16[16,1,128,128]{3,2,1,0:T(8,128)(2,1)} %copy.106), calls=%async_computation.10 | async-start | bytes 1048576 | tf_op jit(solution)/shard_map/all_to_all | solution.py:51
  146.2 73.1 %all-to-all-start.3 = ((f32[16,1,2,3072]{3,2,1,0:T(2,128)}), f32[16,1,2,3072]{3,2,1,0:T(2,128)}, u32[]{:S(2)}, u32[]{:S(2)}) async-start(f32[16,1,2,3072]{3,2,1,0:T(2,128)} %broadcast_in_dim.35), calls=%async_computation.3 | async-start | bytes 786432 | tf_op jit(solution)/shard_map/all_to_all | solution.py:19
  151.5 5.4 %copy-start.3 = (bf16[4,1,512,128]{3,2,0,1:T(8,128)(2,1)}, bf16[4,1,512,128]{3,2,0,1:T(8,128)(2,1)S(1)}, u32[]{:S(2)}) copy-start(bf16[4,1,512,128]{3,2,0,1:T(8,128)(2,1)S(1)} %get-tuple-element.278) | copy-start | bytes 1572868 | tf_op jit(solution)/shard_map/while
  157.1 3.5 %copy-start = (f32[512,2048]{1,0:T(8,128)S(1)}, f32[512,2048]{1,0:T(8,128)}, u32[]{:S(2)}) copy-start(f32[512,2048]{1,0:T(8,128)} %fusion.71) | copy-start | bytes 12582916 | tf_op jit(solution)/shard_map/while
  161.3 4.2 %copy-start.1 = (f32[512,2048]{1,0:T(8,128)S(1)}, f32[512,2048]{1,0:T(8,128)}, u32[]{:S(2)}) copy-start(f32[512,2048]{1,0:T(8,128)} %fusion.71) | copy-start | bytes 12582916 | tf_op jit(solution)/shard_map/while
  165.4 1.8 copy-start.4
  167.2 5.4 %copy-start.3 = (bf16[4,1,512,128]{3,2,0,1:T(8,128)(2,1)}, bf16[4,1,512,128]{3,2,0,1:T(8,128)(2,1)S(1)}, u32[]{:S(2)}) copy-start(bf16[4,1,512,128]{3,2,0,1:T(8,128)(2,1)S(1)} %get-tuple-element.278) | copy-start | bytes 1572868 | tf_op jit(solution)/shard_map/while
  172.8 3.5 %copy-start = (f32[512,2048]{1,0:T(8,128)S(1)}, f32[512,2048]{1,0:T(8,128)}, u32[]{:S(2)}) copy-start(f32[512,2048]{1,0:T(8,128)} %fusion.71) | copy-start | bytes 12582916 | tf_op jit(solution)/shard_map/while
  177.0 4.5 %copy-start.1 = (f32[512,2048]{1,0:T(8,128)S(1)}, f32[512,2048]{1,0:T(8,128)}, u32[]{:S(2)}) copy-start(f32[512,2048]{1,0:T(8,128)} %fusion.71) | copy-start | bytes 12582916 | tf_op jit(solution)/shard_map/while
  181.5 3.1 copy-start.4
  184.6 5.4 %copy-start.3 = (bf16[4,1,512,128]{3,2,0,1:T(8,128)(2,1)}, bf16[4,1,512,128]{3,2,0,1:T(8,128)(2,1)S(1)}, u32[]{:S(2)}) copy-start(bf16[4,1,512,128]{3,2,0,1:T(8,128)(2,1)S(1)} %get-tuple-element.278) | copy-start | bytes 1572868 | tf_op jit(solution)/shard_map/while
  190.1 3.5 %copy-start = (f32[512,2048]{1,0:T(8,128)S(1)}, f32[512,2048]{1,0:T(8,128)}, u32[]{:S(2)}) copy-start(f32[512,2048]{1,0:T(8,128)} %fusion.71) | copy-start | bytes 12582916 | tf_op jit(solution)/shard_map/while
  194.3 4.5 %copy-start.1 = (f32[512,2048]{1,0:T(8,128)S(1)}, f32[512,2048]{1,0:T(8,128)}, u32[]{:S(2)}) copy-start(f32[512,2048]{1,0:T(8,128)} %fusion.71) | copy-start | bytes 12582916 | tf_op jit(solution)/shard_map/while
  198.8 3.1 copy-start.4
  201.9 5.4 %copy-start.3 = (bf16[4,1,512,128]{3,2,0,1:T(8,128)(2,1)}, bf16[4,1,512,128]{3,2,0,1:T(8,128)(2,1)S(1)}, u32[]{:S(2)}) copy-start(bf16[4,1,512,128]{3,2,0,1:T(8,128)(2,1)S(1)} %get-tuple-element.278) | copy-start | bytes 1572868 | tf_op jit(solution)/shard_map/while
  207.4 3.5 %copy-start = (f32[512,2048]{1,0:T(8,128)S(1)}, f32[512,2048]{1,0:T(8,128)}, u32[]{:S(2)}) copy-start(f32[512,2048]{1,0:T(8,128)} %fusion.71) | copy-start | bytes 12582916 | tf_op jit(solution)/shard_map/while
  211.6 4.5 %copy-start.1 = (f32[512,2048]{1,0:T(8,128)S(1)}, f32[512,2048]{1,0:T(8,128)}, u32[]{:S(2)}) copy-start(f32[512,2048]{1,0:T(8,128)} %fusion.71) | copy-start | bytes 12582916 | tf_op jit(solution)/shard_map/while
  216.2 3.1 copy-start.4
  219.2 29.8 %copy-start.9 = (bf16[4,1,512,128]{3,2,1,0:T(8,128)(2,1)S(1)}, bf16[4,1,512,128]{3,2,1,0:T(8,128)(2,1)}, u32[]{:S(2)}) copy-start(bf16[4,1,512,128]{3,2,1,0:T(8,128)(2,1)} %get-tuple-element.50) | copy-start | bytes 1572868
  224.9 18.3 %all-to-all-start.5 = ((f32[16,2,1,2,96]{4,1,3,2,0:T(2,128)}), f32[16,2,1,2,96]{4,1,3,2,0:T(2,128)S(1)}, u32[]{:S(2)}, u32[]{:S(2)}) async-start(f32[16,2,1,2,96]{4,1,3,2,0:T(2,128)} %copy.95), calls=%async_computation.5 | async-start | bytes 65536 | tf_op jit(solution)/shard_map/all_to_all | solution.py:82
  245.0 18.7 %all-to-all-start.6 = ((f32[32,1,192]{2,1,0:T(1,128)}), f32[32,1,192]{2,1,0:T(1,128)S(1)}, u32[]{:S(2)}, u32[]{:S(2)}) async-start(f32[32,1,192]{2,1,0:T(1,128)} %copy.97), calls=%async_computation.6 | async-start | bytes 65536 | tf_op jit(solution)/shard_map/all_to_all | solution.py:94
  249.3 21.9 %copy-start.6 = (bf16[1,32,3072]{2,1,0:T(8,128)(2,1)S(1)}, bf16[1,32,3072]{2,1,0:T(8,128)(2,1)}, u32[]{:S(2)}) copy-start(bf16[1,32,3072]{2,1,0:T(8,128)(2,1)} %param.13) | copy-start | bytes 589828
  249.3 23.9 %copy-start.10 = (f32[1,192]{1,0:T(1,128)S(1)}, f32[1,192]{1,0:T(1,128)}, u32[]{:S(2)}) copy-start(f32[1,192]{1,0:T(1,128)} %param.10) | copy-start | bytes 2308
  263.8 56.0 %all-to-all-start.11 = ((bf16[1,3,2048,128]{3,1,0,2:T(4,128)(2,1)}), bf16[1,3,2048,128]{3,1,0,2:T(4,128)(2,1)S(1)}, u32[]{:S(2)}, u32[]{:S(2)}) async-start(bf16[1,3,2048,128]{3,1,0,2:T(4,128)(2,1)} %copy.109), calls=%async_computation.11 | async-start | bytes 4194304 | tf_op jit(solution)/shard_map/all_to_all | solution.py:62
where the time goes:
time: 330 us; the launch traced here: 329 us
  waiting for transfers between devices  124 us (38%)
  matrix products  54 us (16%)
  blocking collectives  50.6 us (15%)
  starting transfers between devices  46.1 us (14%)
  local copies, waits for them, and re-layouts  32.9 us (10%)
  other arithmetic  20.2 us (6%)
    all_to_all x4, waiting for transfers between devices, grouped_exchange(): lax.all_to_all(group, axis, split_axis=split_dim, concat_axis=concat_dim,...  49.2 us
    all_to_all x2, blocking collectives, from_everyone(): return lax.all_to_all(copies, axis, split_axis=0, concat_axis=0, tiled=True)  46.9 us
    all_to_all x1, waiting for transfers between devices, sent_together(): lax.all_to_all(both, axis, split_axis=split_dim, concat_axis=concat_dim,...  45.9 us
    all_to_all x4, starting transfers between devices, grouped_exchange(): lax.all_to_all(group, axis, split_axis=split_dim, concat_axis=concat_dim,...  22 us
    all_to_all x1, waiting for transfers between devices, moved_by_axis(): lax.all_to_all(tiles, axes[k], split_axis=k, concat_axis=k, tiled=True)  13.1 us
    dot_general x4, matrix products, one_block(): jnp.einsum('ist,itd->isd', prob_low, value, preferred_element_type=jnp.fl...  12.7 us
    dot_general x4, matrix products, one_block(): jnp.einsum('ist,isd->itd', score_low, query_part, preferred_element_type=...  12.3 us
    all_to_all x1, waiting for transfers between devices, per_device(): lax.all_to_all(summed_scale, DP, split_axis=0, concat_axis=1, tiled=True)  12.2 us
  transfers between devices with their start and end apart: 9, of which 8 were waited for; matrix products, arithmetic and copies ran while one was open for 27% of the time, Pallas kernels for 0%

commit v1 on v0

v1 whole, which is shorter than its diff:
```python
import math

import jax
import jax.numpy as jnp
from jax import lax
from jax.experimental import pallas as pl
from jax.experimental.pallas import tpu as pltpu
from jax.sharding import PartitionSpec as P

HEADS = 16
HEAD_DIM = 128
NORM_EPS = 1e-06
PEERS = 16
BLOCK = 4
CHUNK = 256
LOG2E = math.log2(math.e)
MESH = pl.DeviceIdType.MESH


def place_to(me, s):
    return ((me // 4 + s % 4) % 4) * 4 + (me % 4 + s // 4) % 4


def place_from(me, s):
    return ((me // 4 + 4 - s % 4) % 4) * 4 + (me % 4 + 4 - s // 4) % 4


def nt(a, b):
    return lax.dot_general(a, b, (((1,), (1,)), ((), ())), preferred_element_type=jnp.float32)


def nn(a, b):
    return lax.dot_general(a, b, (((1,), (0,)), ((), ())), preferred_element_type=jnp.float32)


def attention_kernel(
    q_ref, k_ref, v_ref, g_ref, dq_ref, dk_ref, dv_ref,
    qb, kb, vb, gb, kt, u, dp, dka, dva, dqo, dko, dvo, send, recv, local,
):
    rows = q_ref.shape[0]
    width = qb.shape[2]
    tokens = PEERS * rows
    chunks = tokens // CHUNK
    block = BLOCK * rows
    factor = width ** (-0.5)
    me = lax.axis_index("seq")

    def head_of(device):
        return pl.ds(pl.multiple_of(device * width, width), width)

    ins = ((k_ref, kb), (v_ref, vb), (q_ref, qb), (g_ref, gb))
    outs = ((dqo, dq_ref), (dko, dk_ref), (dvo, dv_ref))

    def inward(a, s):
        src, dst = ins[a]
        to = place_to(me, s)
        return pltpu.make_async_remote_copy(
            src.at[:, head_of(to)], dst.at[s], send.at[a, s], recv.at[a, s],
            device_id={"seq": to}, device_id_type=MESH,
        )

    def outward(a, s):
        src, dst = outs[a]
        return pltpu.make_async_remote_copy(
            src.at[s], dst.at[:, head_of(me)], send.at[4 + a, s], recv.at[4 + a, s],
            device_id={"seq": place_from(me, s)}, device_id_type=MESH,
        )

    def own_in(a):
        src, dst = ins[a]
        return pltpu.make_async_copy(src.at[:, head_of(me)], dst.at[0], local.at[a])

    def own_out(a):
        src, dst = outs[a]
        return pltpu.make_async_copy(src.at[0], dst.at[:, head_of(me)], local.at[4 + a])

    for a in range(4):
        own_in(a).start()

    barrier = pltpu.get_barrier_semaphore()

    @pl.loop(1, PEERS)
    def _(s):
        pl.semaphore_signal(
            barrier, inc=1, device_id={"seq": place_to(me, s)}, device_id_type=MESH
        )

    pl.semaphore_wait(barrier, PEERS - 1)

    for group in ((0,), (1,), (2, 3)):

        @pl.loop(1, PEERS)
        def _(s):
            for a in group:
                inward(a, s).start()

    dka[...] = jnp.zeros_like(dka)
    dva[...] = jnp.zeros_like(dva)
    for a in range(4):
        own_in(a).wait()

    @pl.loop(1, PEERS)
    def _(s):
        inward(0, s).wait_recv()

    for s in range(PEERS):
        kt[:, s * rows : (s + 1) * rows] = kb[s].astype(jnp.float32).T.astype(jnp.bfloat16)

    @pl.loop(1, PEERS)
    def _(s):
        inward(1, s).wait_recv()

    per_chunk = CHUNK // rows

    @pl.loop(0, PEERS // BLOCK)
    def _(i):
        first = i * BLOCK
        for j in range(BLOCK):

            @pl.when(first + j > 0)
            def _():
                inward(2, first + j).wait_recv()
                inward(3, first + j).wait_recv()

        here = pl.ds(pl.multiple_of(first, BLOCK), BLOCK)
        queries = qb[here].reshape(block, width)
        grads = gb[here].reshape(block, width)
        peak = None
        for t in range(chunks):
            keys = kb[t * per_chunk : (t + 1) * per_chunk].reshape(CHUNK, width)
            scores = nt(keys, queries)
            u[t] = scores
            top = jnp.max(scores.reshape(CHUNK // 8, 8, block), axis=0)
            peak = top if peak is None else jnp.maximum(peak, top)
        peak = jnp.max(peak, axis=0, keepdims=True)
        total = jnp.zeros((8, block), jnp.float32)
        delta = jnp.zeros((8, block), jnp.float32)
        for t in range(chunks):
            values = vb[t * per_chunk : (t + 1) * per_chunk].reshape(CHUNK, width)
            prob_grad = nt(values, grads)
            exponent = jnp.exp2((u[t] - peak) * (factor * LOG2E))
            total += jnp.sum(exponent.reshape(CHUNK // 8, 8, block), axis=0)
            delta += jnp.sum((exponent * prob_grad).reshape(CHUNK // 8, 8, block), axis=0)
            u[t] = exponent
            dp[t] = prob_grad
        inverse = 1.0 / jnp.sum(total, axis=0, keepdims=True)
        delta = jnp.sum(delta, axis=0, keepdims=True) * inverse
        query_grad = jnp.zeros((width, block), jnp.float32)
        for t in range(chunks):
            at = slice(t * CHUNK, (t + 1) * CHUNK)
            probability = u[t] * inverse
            score_low = (probability * (dp[t] - delta)).astype(jnp.bfloat16)
            dva[at] += nn(probability.astype(jnp.bfloat16), grads)
            dka[at] += nn(score_low, queries)
            query_grad += nn(kt[:, at], score_low)
        dqo[here] = (
            (query_grad * factor).T.astype(jnp.bfloat16).reshape(BLOCK, rows, width)
        )
        for j in range(BLOCK):

            @pl.when(first + j > 0)
            def _():
                outward(0, first + j).start()

    own_out(0).start()
    for s in range(PEERS):
        at = slice(s * rows, (s + 1) * rows)
        dko[s] = (dka[at] * factor).astype(jnp.bfloat16)
        dvo[s] = dva[at].astype(jnp.bfloat16)

    @pl.loop(1, PEERS)
    def _(s):
        outward(1, s).start()
        outward(2, s).start()

    own_out(1).start()
    own_out(2).start()

    @pl.loop(1, PEERS)
    def _(s):
        for a in range(4):
            inward(a, s).wait_send()
        for a in range(3):
            outward(a, s).wait_send()

    for a in range(3):
        own_out(a).wait()

    @pl.loop(1, PEERS)
    def _(s):
        for a in range(3):
            outward(a, s).wait_recv()


def attention(q, k, v, g):
    rows, width = q.shape
    slots = pltpu.VMEM((PEERS, rows, HEAD_DIM), jnp.bfloat16)
    tokens = PEERS * rows
    scores = pltpu.VMEM((tokens // CHUNK, CHUNK, BLOCK * rows), jnp.float32)
    total = pltpu.VMEM((tokens, HEAD_DIM), jnp.float32)
    anywhere = pl.BlockSpec(memory_space=pl.ANY)
    return pl.pallas_call(
        attention_kernel,
        out_shape=[jax.ShapeDtypeStruct((rows, width), jnp.bfloat16)] * 3,
        in_specs=[anywhere] * 4,
        out_specs=[anywhere] * 3,
        scratch_shapes=[
            slots, slots, slots, slots,
            pltpu.VMEM((HEAD_DIM, tokens), jnp.bfloat16),
            scores, scores, total, total,
            slots, slots, slots,
            pltpu.SemaphoreType.DMA((7, PEERS)),
            pltpu.SemaphoreType.DMA((7, PEERS)),
            pltpu.SemaphoreType.DMA((7,)),
        ],
        compiler_params=pltpu.CompilerParams(
            collective_id=0, has_side_effects=True, vmem_limit_bytes=50 * 2**20
        ),
        cost_estimate=pl.CostEstimate(
            flops=10 * tokens * tokens * HEAD_DIM,
            bytes_accessed=14 * rows * width,
            transcendentals=tokens * tokens,
        ),
    )(q, k, v, g)


def from_everyone(x, axis):
    copies = jnp.broadcast_to(x, (lax.axis_size(axis), *x.shape))
    return lax.all_to_all(copies, axis, split_axis=0, concat_axis=0, tiled=True)


def split_up(x, dim, devices):
    shape = x.shape
    tiles = x.reshape(*shape[:dim], devices, shape[dim] // devices, *shape[dim + 1 :])
    return jnp.moveaxis(tiles, dim, 0)


def per_device(cond_vec, mod_weight, text_hidden, text_grad, queries, keys, values, out_grad):
    query_grad, key_grad, value_grad = attention(queries[0], keys[0], values[0], out_grad[0])
    cond_all = from_everyone(cond_vec, "dp")[:, 0]
    act = jax.nn.silu(cond_all).astype(jnp.bfloat16)
    partial_scale = jnp.dot(act, mod_weight[1], preferred_element_type=jnp.float32)
    summed_scale = jnp.sum(from_everyone(partial_scale, "seq"), axis=0)
    mod_scale = lax.all_to_all(summed_scale, "dp", split_axis=0, concat_axis=1, tiled=True)
    hidden = text_hidden.astype(jnp.float32)
    incoming = text_grad.astype(jnp.float32)
    centred = hidden - jnp.mean(hidden, axis=-1, keepdims=True)
    inv_std = lax.rsqrt(jnp.mean(centred * centred, axis=-1, keepdims=True) + NORM_EPS)
    normed = centred * inv_std
    grad_mod = jnp.stack([jnp.sum(incoming, axis=1), jnp.sum(incoming * normed, axis=1)], axis=1)
    upstream = incoming * (1.0 + mod_scale[:, None, :])
    text_hidden_grad = inv_std * (
        upstream
        - jnp.mean(upstream, axis=-1, keepdims=True)
        - normed * jnp.mean(upstream * normed, axis=-1, keepdims=True)
    )
    text_hidden_grad = text_hidden_grad.astype(jnp.bfloat16)
    summed_grad = jnp.sum(from_everyone(grad_mod, "seq"), axis=0)
    tiles = split_up(summed_grad, 2, lax.axis_size("dp"))
    owner_grad = lax.all_to_all(tiles, "dp", split_axis=0, concat_axis=0, tiled=True)[:, 0]
    mod_weight_grad = jnp.einsum(
        "br,bkc->krc", act.astype(jnp.float32), owner_grad, precision=lax.Precision.HIGHEST
    )
    backward = jnp.einsum(
        "bkc,krc->br", owner_grad, mod_weight.astype(jnp.float32), precision=lax.Precision.HIGHEST
    )
    arrived = lax.all_to_all(backward, "dp", split_axis=0, concat_axis=0, tiled=True)
    summed_back = arrived.sum(axis=0, keepdims=True)
    sigma = jax.nn.sigmoid(cond_vec)
    cond_vec_grad = summed_back * sigma * (1.0 + cond_vec * (1.0 - sigma))
    return (
        text_hidden_grad, mod_weight_grad, cond_vec_grad,
        query_grad[None], key_grad[None], value_grad[None],
    )


def solution(mesh):
    tokens = P("dp", "seq", None)
    weights = P(None, "seq", "dp")
    return jax.shard_map(
        per_device,
        mesh=mesh,
        in_specs=(P("dp", "seq"), weights, tokens, tokens, tokens, tokens, tokens, tokens),
        out_specs=(tokens, weights, P("dp", "seq"), tokens, tokens, tokens),
        check_vma=False,
    )
```

time: 330 us -> 218 us (0.66)
  the two profiles are of different devices: /device:TPU:64 before, /device:TPU:1 now
where the time goes in v1:
time: 218 us; the launch traced here: 217 us
  Pallas kernels  93.3 us (43%)
  waiting for transfers between devices  50.3 us (23%)
  blocking collectives  33.7 us (15%)
  starting transfers between devices  23.5 us (11%)
  local copies, waits for them, and re-layouts  10.4 us (5%)
  other arithmetic  4.51 us (2%)
    pallas_call x1, Pallas kernels, attention(): pl.pallas_call(attention_kernel, out_shape=[jax.ShapeDtypeStruct((rows, w...  93.3 us
    all_to_all x1, blocking collectives, from_everyone(): return lax.all_to_all(copies, axis, split_axis=0, concat_axis=0, tiled=True)  33.7 us
    all_to_all x1, waiting for transfers between devices, per_device(): lax.all_to_all(summed_scale, 'dp', split_axis=0, concat_axis=1, tiled=True)  14.2 us
    all_to_all x1, waiting for transfers between devices, per_device(): lax.all_to_all(backward, 'dp', split_axis=0, concat_axis=0, tiled=True)  13.5 us
    all_to_all x1, waiting for transfers between devices, per_device(): lax.all_to_all(tiles, 'dp', split_axis=0, concat_axis=0, tiled=True)[:, 0]  13.1 us
    all_to_all x2, starting transfers between devices, from_everyone(): return lax.all_to_all(copies, axis, split_axis=0, concat_axis=0, tiled=True)  9.79 us
    all_to_all x2, waiting for transfers between devices, from_everyone(): return lax.all_to_all(copies, axis, split_axis=0, concat_axis=0, tiled=True)  9.49 us
    unnamed x36, local copies, waits for them, and re-layouts  7.4 us
  transfers between devices with their start and end apart: 5, of which 4 were waited for; matrix products, arithmetic and copies ran while one was open for 1% of the time, Pallas kernels for 43%

profile of v1, /device:TPU:1, one launch (start us, length us, event | category | flops | bytes accessed | tf_op | source)
XLA Modules:
  0.0 217.3 jit_solution(5261911774787581034)
XLA Ops:
  0.6 0.0 copy-start.10
  0.6 0.0 copy-start.8
  0.7 0.7 copy-done.10
  1.3 33.7 %all_to_all.42 = f32[32,1,192]{2,1,0:T(1,128)S(1)} all-to-all(f32[32,1,192]{2,1,0:T(1,128)S(1)} %broadcast_in_dim.26), channel_id=1, replica_groups=mesh['dp'=32,'seq'=16] {'dp'}, dimensions={0} | all-to-all | bytes 49152 | tf_op jit(solution)/shard_map/all_to_all | solution.py:229
  35.0 0.1 fusion.12
  35.2 0.5 copy-done.6
  35.6 0.7 broadcast_in_dim.27
  36.4 5.6 %all-to-all-start.1 = ((f32[16,32,96]{2,1,0:T(8,128)}), f32[16,32,96]{2,1,0:T(8,128)S(1)}, u32[]{:S(2)}, u32[]{:S(2)}) async-start(f32[16,32,96]{2,1,0:T(8,128)} %broadcast_in_dim.27), calls=%async_computation.1 | async-start | bytes 524288 | tf_op jit(solution)/shard_map/all_to_all | solution.py:229
  42.0 0.1 convert_reduce_fusion.1
  42.1 0.2 fusion.9
  42.4 9.5 %all-to-all-done.1 = f32[16,32,96]{2,1,0:T(8,128)S(1)} async-done(((f32[16,32,96]{2,1,0:T(8,128)}), f32[16,32,96]{2,1,0:T(8,128)S(1)}, u32[]{:S(2)}, u32[]{:S(2)}) %all-to-all-start.1) | async-done | bytes 196640 | tf_op jit(solution)/shard_map/all_to_all | solution.py:229
  51.9 0.6 reduce_sum.83
  52.5 5.2 %all-to-all-start.2 = ((f32[32,1,96]{2,1,0:T(1,128)}), f32[32,1,96]{2,1,0:T(1,128)S(1)}, u32[]{:S(2)}, u32[]{:S(2)}) async-start(f32[32,1,96]{2,1,0:T(1,128)} %bitcast.4), calls=%async_computation.2 | async-start | bytes 32768 | tf_op jit(solution)/shard_map/all_to_all | solution.py:244
  57.7 0.0 copy-start.12
  57.7 14.2 %all-to-all-done.2 = f32[32,1,96]{2,1,0:T(1,128)S(1)} async-done(((f32[32,1,96]{2,1,0:T(1,128)}), f32[32,1,96]{2,1,0:T(1,128)S(1)}, u32[]{:S(2)}, u32[]{:S(2)}) %all-to-all-start.2) | async-done | bytes 12320 | tf_op jit(solution)/shard_map/all_to_all | solution.py:244
  72.0 0.1 add.42
  72.1 0.0 copy-start.2
  72.1 0.8 fusion.11
  72.9 0.0 copy-start
  72.9 0.0 copy-start.1
  72.9 0.8 broadcast_in_dim.28
  73.8 4.2 %all-to-all-start.3 = ((f32[16,1,2,3072]{3,2,1,0:T(2,128)}), f32[16,1,2,3072]{3,2,1,0:T(2,128)}, u32[]{:S(2)}, u32[]{:S(2)}) async-start(f32[16,1,2,3072]{3,2,1,0:T(2,128)} %broadcast_in_dim.28), calls=%async_computation.3 | async-start | bytes 786432 | tf_op jit(solution)/shard_map/all_to_all | solution.py:229
  78.0 0.0 copy-start.3
  78.0 1.0 copy-done.3
  79.1 93.3 %shard_map.130 = (bf16[128,2048]{1,0:T(8,128)(2,1)S(1)}, bf16[128,2048]{1,0:T(8,128)(2,1)S(1)}, bf16[128,2048]{1,0:T(8,128)(2,1)S(1)}) custom-call(bf16[128,2048]{1,0:T(8,128)(2,1)S(1)} %bitcast.40, bf16[128,2048]{1,0:T(8,128)(2,1)S(1)} %bitcast.41, bf16[128,2048]{1,0:T(8,128)(2,1)S(1)} %bitcast.42, bf16[128,2048]{1,0:T(8,128)(2,1)S(1)} %bitcast.43), custom_call_target="tpu_custom_call" | custom-call | flops 5368709120 | bytes 3670016 | tf_op jit(solution)/shard_map/pallas_call | solution.py:202
  172.3 0.0 copy-start.14
  172.4 0.6 copy-done.14
  173.0 0.0 copy-done.15
  173.0 1.1 reduce_sum.88
  174.2 0.1 reshape.85
  174.2 0.6 copy.35
  174.9 4.5 %all-to-all-start.4 = ((f32[32,1,2,96]{3,2,1,0:T(2,128)}), f32[32,1,2,96]{3,2,1,0:T(2,128)S(1)}, u32[]{:S(2)}, u32[]{:S(2)}) async-start(f32[32,1,2,96]{3,2,1,0:T(2,128)} %copy.35), calls=%async_computation.4 | async-start | bytes 65536 | tf_op jit(solution)/shard_map/all_to_all | solution.py:260
  179.4 0.0 copy-start.13
  179.4 0.6 copy-done.13
  180.0 0.8 fusion.8
  180.9 13.1 %all-to-all-done.4 = f32[32,1,2,96]{3,2,1,0:T(2,128)S(1)} async-done(((f32[32,1,2,96]{3,2,1,0:T(2,128)}), f32[32,1,2,96]{3,2,1,0:T(2,128)S(1)}, u32[]{:S(2)}, u32[]{:S(2)}) %all-to-all-start.4) | async-done | bytes 24608 | tf_op jit(solution)/shard_map/all_to_all | solution.py:260
  194.0 0.2 convolution_bitcast_fusion.1
  194.2 0.6 copy.37
  194.9 4.0 %all-to-all-start.5 = ((f32[32,1,192]{2,1,0:T(1,128)}), f32[32,1,192]{2,1,0:T(1,128)S(1)}, u32[]{:S(2)}, u32[]{:S(2)}) async-start(f32[32,1,192]{2,1,0:T(1,128)} %copy.37), calls=%async_computation.5 | async-start | bytes 65536 | tf_op jit(solution)/shard_map/all_to_all | solution.py:267
  198.9 0.3 convolution_bitcast_fusion
  199.2 0.8 copy.38
  200.0 13.5 %all-to-all-done.5 = f32[32,1,192]{2,1,0:T(1,128)S(1)} async-done(((f32[32,1,192]{2,1,0:T(1,128)}), f32[32,1,192]{2,1,0:T(1,128)S(1)}, u32[]{:S(2)}, u32[]{:S(2)}) %all-to-all-start.5) | async-done | bytes 24608 | tf_op jit(solution)/shard_map/all_to_all | solution.py:267
  213.6 0.1 reduce_sum.89
  213.6 0.7 copy-done.11
  214.3 0.6 add_multiply_fusion
  214.9 0.8 copy.58
  215.7 0.8 copy.59
  216.5 0.8 copy.60
  (23 shorter events, 0.1 us)
Async XLA Ops:
  0.6 0.7 copy-start.10
  0.6 34.4 %copy-start.8 = (bf16[2,192,96]{2,1,0:T(8,128)(2,1)S(1)}, bf16[2,192,96]{2,1,0:T(8,128)(2,1)}, u32[]{:S(2)}) copy-start(bf16[2,192,96]{2,1,0:T(8,128)(2,1)} %param.9) | copy-start | bytes 221188
  35.0 0.6 copy-start.6
  36.4 5.6 %copy-start.4 = (bf16[1,32,3072]{2,1,0:T(8,128)(2,1)S(1)}, bf16[1,32,3072]{2,1,0:T(8,128)(2,1)}, u32[]{:S(2)}) copy-start(bf16[1,32,3072]{2,1,0:T(8,128)(2,1)} %param.10) | copy-start | bytes 589828
  36.4 15.5 %all-to-all-start.1 = ((f32[16,32,96]{2,1,0:T(8,128)}), f32[16,32,96]{2,1,0:T(8,128)S(1)}, u32[]{:S(2)}, u32[]{:S(2)}) async-start(f32[16,32,96]{2,1,0:T(8,128)} %broadcast_in_dim.27), calls=%async_computation.1 | async-start | bytes 524288 | tf_op jit(solution)/shard_map/all_to_all | solution.py:229
  42.4 29.7 %copy-start.5 = (bf16[1,32,3072]{2,1,0:T(8,128)(2,1)S(1)}, bf16[1,32,3072]{2,1,0:T(8,128)(2,1)}, u32[]{:S(2)}) copy-start(bf16[1,32,3072]{2,1,0:T(8,128)(2,1)} %param.11) | copy-start | bytes 589828
  52.5 19.4 %all-to-all-start.2 = ((f32[32,1,96]{2,1,0:T(1,128)}), f32[32,1,96]{2,1,0:T(1,128)S(1)}, u32[]{:S(2)}, u32[]{:S(2)}) async-start(f32[32,1,96]{2,1,0:T(1,128)} %bitcast.4), calls=%async_computation.2 | async-start | bytes 32768 | tf_op jit(solution)/shard_map/all_to_all | solution.py:244
  57.7 14.3 %copy-start.12 = (f32[32]{0:T(128)}, f32[32]{0:T(128)S(1)}, u32[]{:S(2)}) copy-start(f32[32]{0:T(128)S(1)} %add_rsqrt_fusion) | copy-start | bytes 388
  72.1 5.9 %copy-start.2 = (bf16[1,128,2048]{2,1,0:T(8,128)(2,1)S(1)}, bf16[1,128,2048]{2,1,0:T(8,128)(2,1)}, u32[]{:S(2)}) copy-start(bf16[1,128,2048]{2,1,0:T(8,128)(2,1)} %param.14) | copy-start | bytes 1572868
  72.9 5.1 %copy-start = (bf16[1,128,2048]{2,1,0:T(8,128)(2,1)S(1)}, bf16[1,128,2048]{2,1,0:T(8,128)(2,1)}, u32[]{:S(2)}) copy-start(bf16[1,128,2048]{2,1,0:T(8,128)(2,1)} %param.12) | copy-start | bytes 1572868
  72.9 5.1 %copy-start.1 = (bf16[1,128,2048]{2,1,0:T(8,128)(2,1)S(1)}, bf16[1,128,2048]{2,1,0:T(8,128)(2,1)}, u32[]{:S(2)}) copy-start(bf16[1,128,2048]{2,1,0:T(8,128)(2,1)} %param.13) | copy-start | bytes 1572868
  73.8 99.3 %all-to-all-start.3 = ((f32[16,1,2,3072]{3,2,1,0:T(2,128)}), f32[16,1,2,3072]{3,2,1,0:T(2,128)}, u32[]{:S(2)}, u32[]{:S(2)}) async-start(f32[16,1,2,3072]{3,2,1,0:T(2,128)} %broadcast_in_dim.28), calls=%async_computation.3 | async-start | bytes 786432 | tf_op jit(solution)/shard_map/all_to_all | solution.py:229
  78.0 1.0 copy-start.3
  172.3 0.7 copy-start.14
  172.4 0.7 copy-start.15
  174.9 19.1 %all-to-all-start.4 = ((f32[32,1,2,96]{3,2,1,0:T(2,128)}), f32[32,1,2,96]{3,2,1,0:T(2,128)S(1)}, u32[]{:S(2)}, u32[]{:S(2)}) async-start(f32[32,1,2,96]{3,2,1,0:T(2,128)} %copy.35), calls=%async_computation.4 | async-start | bytes 65536 | tf_op jit(solution)/shard_map/all_to_all | solution.py:260
  179.4 0.7 copy-start.13
  180.0 14.0 %copy-start.9 = (bf16[2,192,96]{2,1,0:T(8,128)(2,1)S(1)}, bf16[2,192,96]{2,1,0:T(8,128)(2,1)}, u32[]{:S(2)}) copy-start(bf16[2,192,96]{2,1,0:T(8,128)(2,1)} %param.9) | copy-start | bytes 221188
  194.9 4.0 %copy-start.7 = (f32[32,1,192]{2,1,0:T(1,128)S(1)}, f32[32,1,192]{2,1,0:T(1,128)}, u32[]{:S(2)}) copy-start(f32[32,1,192]{2,1,0:T(1,128)} %copy-done.6) | copy-start | bytes 73732
  194.9 18.7 %all-to-all-start.5 = ((f32[32,1,192]{2,1,0:T(1,128)}), f32[32,1,192]{2,1,0:T(1,128)S(1)}, u32[]{:S(2)}, u32[]{:S(2)}) async-start(f32[32,1,192]{2,1,0:T(1,128)} %copy.37), calls=%async_computation.5 | async-start | bytes 65536 | tf_op jit(solution)/shard_map/all_to_all | solution.py:267
  213.6 0.7 copy-start.11

commit v2 on v1

--- a/solution.py
+++ b/solution.py
@@ -11,6 +11,8 @@
 HEAD_DIM = 128
 NORM_EPS = 1e-06
 PEERS = 16
+SAMPLES = 32
+LANES = 128
 BLOCK = 4
 CHUNK = 256
 LOG2E = math.log2(math.e)
@@ -33,9 +35,12 @@
     return lax.dot_general(a, b, (((1,), (0,)), ((), ())), preferred_element_type=jnp.float32)
 
 
-def attention_kernel(
-    q_ref, k_ref, v_ref, g_ref, dq_ref, dk_ref, dv_ref,
-    qb, kb, vb, gb, kt, u, dp, dka, dva, dqo, dko, dvo, send, recv, local,
+def joint_kernel(
+    cond_ref, weight_ref, hidden_ref, incoming_ref, q_ref, k_ref, v_ref, g_ref,
+    hidden_grad_ref, weight_grad_ref, cond_grad_ref, dq_ref, dk_ref, dv_ref,
+    qb, kb, vb, gb, kt, u, dp, dka, dva, dqo, dko, dvo,
+    cond_own, cond_all, parcel, parcels, partial, share, whole, back, backs, row, normed, spread,
+    send, recv, local, dp_send, dp_recv, seq_send, seq_recv,
 ):
     rows = q_ref.shape[0]
     width = qb.shape[2]
@@ -44,6 +49,10 @@
     block = BLOCK * rows
     factor = width ** (-0.5)
     me = lax.axis_index("seq")
+    mine = lax.axis_index("dp")
+    weight_rows, columns = weight_ref.shape[1:]
+    features = hidden_ref.shape[1]
+    text_rows = hidden_ref.shape[0]
 
     def head_of(device):
         return pl.ds(pl.multiple_of(device * width, width), width)
@@ -74,41 +83,155 @@
         src, dst = outs[a]
         return pltpu.make_async_copy(src.at[0], dst.at[:, head_of(me)], local.at[4 + a])
 
+    def other(r):
+        return (mine + r) % SAMPLES
+
+    def dp_copy(step, r, arriving):
+        src = (cond_own, parcel.at[other(r)], back.at[other(r)])[step]
+        dst = (cond_all, parcels, backs)[step]
+        place = other(r) if arriving else mine
+        return pltpu.make_async_remote_copy(
+            src, dst.at[place], dp_send.at[step, r], dp_recv.at[step, place],
+            device_id={"dp": other(r)}, device_id_type=MESH,
+        )
+
+    def scatter_copy(s):
+        to = place_to(me, s)
+        return pltpu.make_async_remote_copy(
+            parcels.at[pl.ds(to * 2, 2)], partial.at[s], seq_send.at[0, s], seq_recv.at[0, s],
+            device_id={"seq": to}, device_id_type=MESH,
+        )
+
+    def gather_copy(s, arriving):
+        place = place_from(me, s) if arriving else me
+        return pltpu.make_async_remote_copy(
+            share, whole.at[pl.ds(place * 2, 2)], seq_send.at[1, s], seq_recv.at[1, s],
+            device_id={"seq": place_to(me, s)}, device_id_type=MESH,
+        )
+
+    def each(low, high, action):
+        pl.loop(low, high)(action)
+
+    cond_own[...] = jnp.zeros_like(cond_own)
+    cond_own[:, :weight_rows] = cond_ref[...]
     for a in range(4):
         own_in(a).start()
 
     barrier = pltpu.get_barrier_semaphore()
 
+    @pl.loop(1, SAMPLES)
+    def _(r):
+        pl.semaphore_signal(barrier, inc=1, device_id={"dp": other(r)}, device_id_type=MESH)
+
     @pl.loop(1, PEERS)
     def _(s):
         pl.semaphore_signal(
             barrier, inc=1, device_id={"seq": place_to(me, s)}, device_id_type=MESH
         )
 
-    pl.semaphore_wait(barrier, PEERS - 1)
-
-    for group in ((0,), (1,), (2, 3)):
-
-        @pl.loop(1, PEERS)
-        def _(s):
-            for a in group:
-                inward(a, s).start()
+    pl.semaphore_wait(barrier, PEERS + SAMPLES - 2)
+
+    each(1, SAMPLES, lambda r: dp_copy(0, r, False).start())
+    each(1, PEERS, lambda s: inward(0, s).start())
+    each(1, PEERS, lambda s: inward(1, s).start())
+
+    plain = jnp.zeros((8, features), jnp.float32)
+    scaled = jnp.zeros((8, features), jnp.float32)
+    for t in range(0, text_rows, 16):
+        at = slice(t, t + 16)
+        hidden = hidden_ref[at].astype(jnp.float32)
+        incoming = incoming_ref[at].astype(jnp.float32)
+        centred = hidden - jnp.sum(hidden, axis=-1, keepdims=True) * (1.0 / features)
+        variance = jnp.sum(centred * centred, axis=-1, keepdims=True) * (1.0 / features)
+        inv_std = lax.rsqrt(variance + NORM_EPS)
+        norm = centred * inv_std
+        normed[at] = norm
+        spread[at] = jnp.broadcast_to(inv_std, (16, LANES))
+        plain += jnp.sum(incoming.reshape(2, 8, features), axis=0)
+        scaled += jnp.sum((incoming * norm).reshape(2, 8, features), axis=0)
+    plain = jnp.sum(plain, axis=0, keepdims=True)
+    scaled = jnp.sum(scaled, axis=0, keepdims=True)
+    parcel[...] = jnp.zeros_like(parcel)
+    back[...] = jnp.zeros_like(back)
+    for p in range(SAMPLES):
+        at = slice(p * columns, (p + 1) * columns)
+        parcel[p, :, LANES : LANES + columns] = plain[:, at]
+        parcel[p, :, 2 * LANES : 2 * LANES + columns] = scaled[:, at]
+
+    cond_all[mine] = cond_own[...]
+    each(1, SAMPLES, lambda r: dp_copy(0, r, True).wait_recv())
+    cond = cond_all[...].reshape(SAMPLES, cond_all.shape[2])[:, :weight_rows]
+    act = (cond * jax.nn.sigmoid(cond)).astype(jnp.bfloat16)
+    parcel[:, :, :columns] = nn(act, weight_ref[1]).reshape(SAMPLES, 1, columns)
+    each(1, SAMPLES, lambda r: dp_copy(1, r, False).start())
+
+    @pl.loop(1, PEERS)
+    def _(s):
+        inward(2, s).start()
+        inward(3, s).start()
+
+    def scatter_sums():
+        parcels[mine] = parcel[mine]
+        each(1, SAMPLES, lambda r: dp_copy(1, r, True).wait_recv())
+        each(1, PEERS, lambda s: scatter_copy(s).start())
+
+    def gather_sums():
+        partial[0] = parcels[pl.ds(me * 2, 2)]
+        each(1, PEERS, lambda s: scatter_copy(s).wait_recv())
+        share[...] = jnp.sum(partial[...], axis=0)
+        each(1, PEERS, lambda s: gather_copy(s, False).start())
+
+    def weight_gradients():
+        whole[pl.ds(me * 2, 2)] = share[...]
+        each(1, PEERS, lambda s: gather_copy(s, True).wait_recv())
+        sums = whole[...].reshape(SAMPLES, whole.shape[2])
+        cond = cond_all[...].reshape(SAMPLES, cond_all.shape[2])[:, :weight_rows]
+        act = (cond * jax.nn.sigmoid(cond)).astype(jnp.bfloat16).astype(jnp.float32)
+        backward = jnp.zeros((SAMPLES, weight_rows), jnp.float32)
+        for k in range(2):
+            grad = sums[:, (k + 1) * LANES : (k + 1) * LANES + columns]
+            weight_grad_ref[k] = lax.dot_general(
+                act, grad, (((0,), (0,)), ((), ())),
+                precision=lax.Precision.HIGHEST, preferred_element_type=jnp.float32,
+            )
+            backward += lax.dot_general(
+                grad, weight_ref[k].astype(jnp.float32), (((1,), (1,)), ((), ())),
+                precision=lax.Precision.HIGHEST, preferred_element_type=jnp.float32,
+            )
+        back[:, :, :weight_rows] = backward.reshape(SAMPLES, 1, weight_rows)
+        each(1, SAMPLES, lambda r: dp_copy(2, r, False).start())
+
+    def text_gradient():
+        for j in range(SAMPLES):
+            row[:, j * columns : (j + 1) * columns] = whole[j, :, :columns]
+        gain = 1.0 + row[...]
+        for t in range(0, text_rows, 16):
+            at = slice(t, t + 16)
+            norm = normed[at]
+            upstream = incoming_ref[at].astype(jnp.float32) * gain
+            mean = jnp.sum(upstream, axis=-1, keepdims=True) * (1.0 / features)
+            along = jnp.sum(upstream * norm, axis=-1, keepdims=True) * (1.0 / features)
+            grad = spread[at, :1] * (upstream - mean - norm * along)
+            hidden_grad_ref[at] = grad.astype(jnp.bfloat16)
+
+    def cond_gradient():
+        backs[mine] = back[mine]
+        each(1, SAMPLES, lambda r: dp_copy(2, r, True).wait_recv())
+        summed = jnp.sum(backs[...], axis=0)[:, :weight_rows]
+        cond = cond_ref[...]
+        sigma = jax.nn.sigmoid(cond)
+        cond_grad_ref[...] = summed * sigma * (1.0 + cond * (1.0 - sigma))
 
     dka[...] = jnp.zeros_like(dka)
     dva[...] = jnp.zeros_like(dva)
     for a in range(4):
         own_in(a).wait()
-
-    @pl.loop(1, PEERS)
-    def _(s):
-        inward(0, s).wait_recv()
+    each(1, PEERS, lambda s: inward(0, s).wait_recv())
 
     for s in range(PEERS):
         kt[:, s * rows : (s + 1) * rows] = kb[s].astype(jnp.float32).T.astype(jnp.bfloat16)
 
-    @pl.loop(1, PEERS)
-    def _(s):
-        inward(1, s).wait_recv()
+    each(1, PEERS, lambda s: inward(1, s).wait_recv())
 
     per_chunk = CHUNK // rows
 
@@ -162,6 +285,10 @@
             def _():
                 outward(0, first + j).start()
 
+        pl.when(i == 0)(scatter_sums)
+        pl.when(i == 1)(gather_sums)
+        pl.when(i == 2)(weight_gradients)
+
     own_out(0).start()
     for s in range(PEERS):
         at = slice(s * rows, (s + 1) * rows)
@@ -175,6 +302,18 @@
 
     own_out(1).start()
     own_out(2).start()
+    text_gradient()
+    cond_gradient()
+
+    @pl.loop(1, SAMPLES)
+    def _(r):
+        for step in range(3):
+            dp_copy(step, r, False).wait_send()
+
+    @pl.loop(1, PEERS)
+    def _(s):
+        scatter_copy(s).wait_send()
+        gather_copy(s, False).wait_send()
 
     @pl.loop(1, PEERS)
     def _(s):
@@ -192,26 +331,50 @@
             outward(a, s).wait_recv()
 
 
-def attention(q, k, v, g):
+def joint(cond, weight, hidden, incoming, q, k, v, g):
     rows, width = q.shape
     slots = pltpu.VMEM((PEERS, rows, HEAD_DIM), jnp.bfloat16)
     tokens = PEERS * rows
     scores = pltpu.VMEM((tokens // CHUNK, CHUNK, BLOCK * rows), jnp.float32)
     total = pltpu.VMEM((tokens, HEAD_DIM), jnp.float32)
     anywhere = pl.BlockSpec(memory_space=pl.ANY)
+    inside = pl.BlockSpec(memory_space=pltpu.VMEM)
+    padded = -(-cond.shape[1] // LANES) * LANES
+    f32 = jnp.float32
     return pl.pallas_call(
-        attention_kernel,
-        out_shape=[jax.ShapeDtypeStruct((rows, width), jnp.bfloat16)] * 3,
-        in_specs=[anywhere] * 4,
-        out_specs=[anywhere] * 3,
+        joint_kernel,
+        out_shape=[
+            jax.ShapeDtypeStruct(hidden.shape, jnp.bfloat16),
+            jax.ShapeDtypeStruct(weight.shape, f32),
+            jax.ShapeDtypeStruct(cond.shape, f32),
+        ]
+        + [jax.ShapeDtypeStruct((rows, width), jnp.bfloat16)] * 3,
+        in_specs=[inside] * 4 + [anywhere] * 4,
+        out_specs=[inside] * 3 + [anywhere] * 3,
         scratch_shapes=[
             slots, slots, slots, slots,
             pltpu.VMEM((HEAD_DIM, tokens), jnp.bfloat16),
             scores, scores, total, total,
             slots, slots, slots,
+            pltpu.VMEM((1, padded), f32),
+            pltpu.VMEM((SAMPLES, 1, padded), f32),
+            pltpu.VMEM((SAMPLES, 1, 3 * LANES), f32),
+            pltpu.VMEM((SAMPLES, 1, 3 * LANES), f32),
+            pltpu.VMEM((PEERS, 2, 1, 3 * LANES), f32),
+            pltpu.VMEM((2, 1, 3 * LANES), f32),
+            pltpu.VMEM((SAMPLES, 1, 3 * LANES), f32),
+            pltpu.VMEM((SAMPLES, 1, padded), f32),
+            pltpu.VMEM((SAMPLES, 1, padded), f32),
+            pltpu.VMEM((1, hidden.shape[1]), f32),
+            pltpu.VMEM(hidden.shape, f32),
+            pltpu.VMEM((hidden.shape[0], LANES), f32),
             pltpu.SemaphoreType.DMA((7, PEERS)),
             pltpu.SemaphoreType.DMA((7, PEERS)),
             pltpu.SemaphoreType.DMA((7,)),
+            pltpu.SemaphoreType.DMA((3, SAMPLES)),
+            pltpu.SemaphoreType.DMA((3, SAMPLES)),
+            pltpu.SemaphoreType.DMA((2, PEERS)),
+            pltpu.SemaphoreType.DMA((2, PEERS)),
         ],
         compiler_params=pltpu.CompilerParams(
             collective_id=0, has_side_effects=True, vmem_limit_bytes=50 * 2**20
@@ -221,55 +384,17 @@
             bytes_accessed=14 * rows * width,
             transcendentals=tokens * tokens,
         ),
-    )(q, k, v, g)
-
-
-def from_everyone(x, axis):
-    copies = jnp.broadcast_to(x, (lax.axis_size(axis), *x.shape))
-    return lax.all_to_all(copies, axis, split_axis=0, concat_axis=0, tiled=True)
-
-
-def split_up(x, dim, devices):
-    shape = x.shape
-    tiles = x.reshape(*shape[:dim], devices, shape[dim] // devices, *shape[dim + 1 :])
-    return jnp.moveaxis(tiles, dim, 0)
+    )(cond, weight, hidden, incoming, q, k, v, g)
 
 
 def per_device(cond_vec, mod_weight, text_hidden, text_grad, queries, keys, values, out_grad):
-    query_grad, key_grad, value_grad = attention(queries[0], keys[0], values[0], out_grad[0])
-    cond_all = from_everyone(cond_vec, "dp")[:, 0]
-    act = jax.nn.silu(cond_all).astype(jnp.bfloat16)
-    partial_scale = jnp.dot(act, mod_weight[1], preferred_element_type=jnp.float32)
-    summed_scale = jnp.sum(from_everyone(partial_scale, "seq"), axis=0)
-    mod_scale = lax.all_to_all(summed_scale, "dp", split_axis=0, concat_axis=1, tiled=True)
-    hidden = text_hidden.astype(jnp.float32)
-    incoming = text_grad.astype(jnp.float32)
-    centred = hidden - jnp.mean(hidden, axis=-1, keepdims=True)
-    inv_std = lax.rsqrt(jnp.mean(centred * centred, axis=-1, keepdims=True) + NORM_EPS)
-    normed = centred * inv_std
-    grad_mod = jnp.stack([jnp.sum(incoming, axis=1), jnp.sum(incoming * normed, axis=1)], axis=1)
-    upstream = incoming * (1.0 + mod_scale[:, None, :])
-    text_hidden_grad = inv_std * (
-        upstream
-        - jnp.mean(upstream, axis=-1, keepdims=True)
-        - normed * jnp.mean(upstream * normed, axis=-1, keepdims=True)
+    grads = joint(
+        cond_vec, mod_weight, text_hidden[0], text_grad[0],
+        queries[0], keys[0], values[0], out_grad[0],
     )
-    text_hidden_grad = text_hidden_grad.astype(jnp.bfloat16)
-    summed_grad = jnp.sum(from_everyone(grad_mod, "seq"), axis=0)
-    tiles = split_up(summed_grad, 2, lax.axis_size("dp"))
-    owner_grad = lax.all_to_all(tiles, "dp", split_axis=0, concat_axis=0, tiled=True)[:, 0]
-    mod_weight_grad = jnp.einsum(
-        "br,bkc->krc", act.astype(jnp.float32), owner_grad, precision=lax.Precision.HIGHEST
-    )
-    backward = jnp.einsum(
-        "bkc,krc->br", owner_grad, mod_weight.astype(jnp.float32), precision=lax.Precision.HIGHEST
-    )
-    arrived = lax.all_to_all(backward, "dp", split_axis=0, concat_axis=0, tiled=True)
-    summed_back = arrived.sum(axis=0, keepdims=True)
-    sigma = jax.nn.sigmoid(cond_vec)
-    cond_vec_grad = summed_back * sigma * (1.0 + cond_vec * (1.0 - sigma))
+    hidden_grad, weight_grad, cond_grad, query_grad, key_grad, value_grad = grads
     return (
-        text_hidden_grad, mod_weight_grad, cond_vec_grad,
+        hidden_grad[None], weight_grad, cond_grad,
         query_grad[None], key_grad[None], value_grad[None],
     )
 

time: 218 us -> 129 us (0.59)
  waiting for transfers between devices: 50.3 us -> 0 us
  blocking collectives: 33.7 us -> 0 us
  Pallas kernels: 93.3 us -> 117 us
  starting transfers between devices: 23.5 us -> 0 us
  other arithmetic: 4.51 us -> 0 us
    all_to_all x5 -> x0, waiting for transfers between devices: 50.3 us -> none  [the longest x1 14.2 us: per_device(): lax.all_to_all(summed_scale, 'dp', split_axis=0, concat_axis=1, tiled=True)]
    all_to_all x1 -> x0, blocking collectives: 33.7 us -> none  [from_everyone(): return lax.all_to_all(copies, axis, split_axis=0, concat_axis=0, tiled=True)]
    pallas_call x1, Pallas kernels: 93.3 us -> 117 us  [joint(): pl.pallas_call(joint_kernel, out_shape=[jax.ShapeDtypeStruct(hidden.shape...]
    all_to_all x5 -> x0, starting transfers between devices: 23.5 us -> none  [the longest x2 9.79 us: from_everyone(): return lax.all_to_all(copies, axis, split_axis=0, concat_axis=0, tiled=True)]
    unnamed x36 -> x20, local copies, waits for them, and re-layouts: 7.4 us -> 10.8 us
    reduce_sum x6 -> x0, other arithmetic: 2.99 us -> none  [the longest x1 1.12 us: per_device(): summed_grad = jnp.sum(from_everyone(grad_mod, 'seq'), axis=0)]
  transfers between devices with their start and end apart: 5 -> 0, of which waited for: 4 -> 0; matrix products, arithmetic and copies ran while one was open for 1% -> 0% of each run, Pallas kernels for 43% -> 0%
where the time goes in v2:
time: 129 us
  Pallas kernels  117 us (91%)
  local copies, waits for them, and re-layouts  10.8 us (8%)
    pallas_call x1, Pallas kernels, joint(): pl.pallas_call(joint_kernel, out_shape=[jax.ShapeDtypeStruct(hidden.shape...  117 us
    unnamed x20, local copies, waits for them, and re-layouts  10.8 us

profile of v2, /device:TPU:1, one launch (start us, length us, event | category | flops | bytes accessed | tf_op | source)
XLA Modules:
  0.0 128.6 jit_solution(2811023553203788918)
XLA Ops:
  0.6 0.0 copy-start.6
  0.6 0.7 copy-done.6
  1.3 0.0 copy-start
  1.3 1.0 copy-done
  2.4 0.0 copy-start.1
  2.4 1.0 copy-done.1
  3.4 0.0 copy-start.2
  3.4 1.0 copy-done.2
  4.4 0.0 copy-start.3
  4.4 0.9 copy-done.3
  5.4 0.0 copy-start.4
  5.4 0.9 copy-done.4
  6.3 0.0 copy-start.5
  6.3 0.9 copy-done.5
  7.2 117.1 %shard_map.127 = (bf16[32,3072]{1,0:T(8,128)(2,1)S(1)}, f32[2,192,96]{2,1,0:T(8,128)S(1)}, f32[1,192]{1,0:T(1,128)S(1)}, bf16[128,2048]{1,0:T(8,128)(2,1)S(1)}, ...) custom-call(f32[1,192]{1,0:T(1,128)S(1)} %copy-done.6, bf16[2,192,96]{2,1,0:T(8,128)(2,1)S(1)} %copy-done.5, ...), custom_call_target="tpu_custom_call" | custom-call | flops 5368709120 | bytes 3670016 | tf_op jit(solution)/shard_map/pallas_call | solution.py:344
  124.3 0.7 copy.20
  124.9 0.7 copy.21
  125.6 0.6 copy.22
  126.2 0.8 copy.23
  127.0 0.8 copy.24
  127.8 0.8 copy.25
Async XLA Ops:
  0.6 0.7 copy-start.6
  1.3 1.0 copy-start
  2.4 1.0 copy-start.1
  3.4 1.0 copy-start.2
  4.4 0.9 copy-start.3
  5.4 0.9 copy-start.4
  6.3 0.9 copy-start.5

commit v3 on v2

--- a/solution.py
+++ b/solution.py
@@ -36,8 +36,9 @@
 
 
 def joint_kernel(
-    cond_ref, weight_ref, hidden_ref, incoming_ref, q_ref, k_ref, v_ref, g_ref,
-    hidden_grad_ref, weight_grad_ref, cond_grad_ref, dq_ref, dk_ref, dv_ref,
+    cond_in, weight_in, hidden_in, incoming_in, q_ref, k_ref, v_ref, g_ref,
+    hidden_grad_out, weight_grad_out, cond_grad_out, dq_ref, dk_ref, dv_ref,
+    cond_ref, weight_ref, hidden_ref, incoming_ref, hidden_grad_ref, weight_grad_ref, cond_grad_ref,
     qb, kb, vb, gb, kt, u, dp, dka, dva, dqo, dko, dvo,
     cond_own, cond_all, parcel, parcels, partial, share, whole, back, backs, row, normed, spread,
     send, recv, local, dp_send, dp_recv, seq_send, seq_recv,
@@ -83,6 +84,17 @@
         src, dst = outs[a]
         return pltpu.make_async_copy(src.at[0], dst.at[:, head_of(me)], local.at[4 + a])
 
+    fetched = ((cond_in, cond_ref), (hidden_in, hidden_ref), (incoming_in, incoming_ref),
+               (weight_in, weight_ref))
+    kept = ((weight_grad_ref, weight_grad_out), (hidden_grad_ref, hidden_grad_out),
+            (cond_grad_ref, cond_grad_out))
+
+    def fetch(a):
+        return pltpu.make_async_copy(*fetched[a], local.at[7 + a])
+
+    def keep(a):
+        return pltpu.make_async_copy(*kept[a], local.at[11 + a])
+
     def other(r):
         return (mine + r) % SAMPLES
 
@@ -112,8 +124,8 @@
     def each(low, high, action):
         pl.loop(low, high)(action)
 
-    cond_own[...] = jnp.zeros_like(cond_own)
-    cond_own[:, :weight_rows] = cond_ref[...]
+    for a in range(4):
+        fetch(a).start()
     for a in range(4):
         own_in(a).start()
 
@@ -129,12 +141,16 @@
             barrier, inc=1, device_id={"seq": place_to(me, s)}, device_id_type=MESH
         )
 
+    cond_own[...] = jnp.zeros_like(cond_own)
+    fetch(0).wait()
+    cond_own[:, :weight_rows] = cond_ref[...]
     pl.semaphore_wait(barrier, PEERS + SAMPLES - 2)
 
     each(1, SAMPLES, lambda r: dp_copy(0, r, False).start())
     each(1, PEERS, lambda s: inward(0, s).start())
-    each(1, PEERS, lambda s: inward(1, s).start())
-
+
+    fetch(1).wait()
+    fetch(2).wait()
     plain = jnp.zeros((8, features), jnp.float32)
     scaled = jnp.zeros((8, features), jnp.float32)
     for t in range(0, text_rows, 16):
@@ -162,13 +178,15 @@
     each(1, SAMPLES, lambda r: dp_copy(0, r, True).wait_recv())
     cond = cond_all[...].reshape(SAMPLES, cond_all.shape[2])[:, :weight_rows]
     act = (cond * jax.nn.sigmoid(cond)).astype(jnp.bfloat16)
+    fetch(3).wait()
     parcel[:, :, :columns] = nn(act, weight_ref[1]).reshape(SAMPLES, 1, columns)
     each(1, SAMPLES, lambda r: dp_copy(1, r, False).start())
-
-    @pl.loop(1, PEERS)
-    def _(s):
-        inward(2, s).start()
-        inward(3, s).start()
+    each(1, PEERS, lambda s: inward(1, s).start())
+
+    def send_block(i):
+        for s in range(max(i * BLOCK, 1), (i + 1) * BLOCK):
+            inward(2, s).start()
+            inward(3, s).start()
 
     def scatter_sums():
         parcels[mine] = parcel[mine]
@@ -198,6 +216,7 @@
                 grad, weight_ref[k].astype(jnp.float32), (((1,), (1,)), ((), ())),
                 precision=lax.Precision.HIGHEST, preferred_element_type=jnp.float32,
             )
+        keep(0).start()
         back[:, :, :weight_rows] = backward.reshape(SAMPLES, 1, weight_rows)
         each(1, SAMPLES, lambda r: dp_copy(2, r, False).start())
 
@@ -213,6 +232,7 @@
             along = jnp.sum(upstream * norm, axis=-1, keepdims=True) * (1.0 / features)
             grad = spread[at, :1] * (upstream - mean - norm * along)
             hidden_grad_ref[at] = grad.astype(jnp.bfloat16)
+        keep(1).start()
 
     def cond_gradient():
         backs[mine] = back[mine]
@@ -221,6 +241,7 @@
         cond = cond_ref[...]
         sigma = jax.nn.sigmoid(cond)
         cond_grad_ref[...] = summed * sigma * (1.0 + cond * (1.0 - sigma))
+        keep(2).start()
 
     dka[...] = jnp.zeros_like(dka)
     dva[...] = jnp.zeros_like(dva)
@@ -231,7 +252,12 @@
     for s in range(PEERS):
         kt[:, s * rows : (s + 1) * rows] = kb[s].astype(jnp.float32).T.astype(jnp.bfloat16)
 
+    scatter_sums()
+    send_block(0)
     each(1, PEERS, lambda s: inward(1, s).wait_recv())
+    gather_sums()
+    send_block(1)
+    send_block(2)
 
     per_chunk = CHUNK // rows
 
@@ -285,9 +311,10 @@
             def _():
                 outward(0, first + j).start()
 
-        pl.when(i == 0)(scatter_sums)
-        pl.when(i == 1)(gather_sums)
-        pl.when(i == 2)(weight_gradients)
+        @pl.when(i == 0)
+        def _():
+            weight_gradients()
+            send_block(3)
 
     own_out(0).start()
     for s in range(PEERS):
@@ -324,6 +351,7 @@
 
     for a in range(3):
         own_out(a).wait()
+        keep(a).wait()
 
     @pl.loop(1, PEERS)
     def _(s):
@@ -338,7 +366,6 @@
     scores = pltpu.VMEM((tokens // CHUNK, CHUNK, BLOCK * rows), jnp.float32)
     total = pltpu.VMEM((tokens, HEAD_DIM), jnp.float32)
     anywhere = pl.BlockSpec(memory_space=pl.ANY)
-    inside = pl.BlockSpec(memory_space=pltpu.VMEM)
     padded = -(-cond.shape[1] // LANES) * LANES
     f32 = jnp.float32
     return pl.pallas_call(
@@ -349,9 +376,16 @@
             jax.ShapeDtypeStruct(cond.shape, f32),
         ]
         + [jax.ShapeDtypeStruct((rows, width), jnp.bfloat16)] * 3,
-        in_specs=[inside] * 4 + [anywhere] * 4,
-        out_specs=[inside] * 3 + [anywhere] * 3,
+        in_specs=[anywhere] * 8,
+        out_specs=[anywhere] * 6,
         scratch_shapes=[
+            pltpu.VMEM(cond.shape, f32),
+            pltpu.VMEM(weight.shape, jnp.bfloat16),
+            pltpu.VMEM(hidden.shape, jnp.bfloat16),
+            pltpu.VMEM(hidden.shape, jnp.bfloat16),
+            pltpu.VMEM(hidden.shape, jnp.bfloat16),
+            pltpu.VMEM(weight.shape, f32),
+            pltpu.VMEM(cond.shape, f32),
             slots, slots, slots, slots,
             pltpu.VMEM((HEAD_DIM, tokens), jnp.bfloat16),
             scores, scores, total, total,
@@ -370,14 +404,14 @@
             pltpu.VMEM((hidden.shape[0], LANES), f32),
             pltpu.SemaphoreType.DMA((7, PEERS)),
             pltpu.SemaphoreType.DMA((7, PEERS)),
-            pltpu.SemaphoreType.DMA((7,)),
+            pltpu.SemaphoreType.DMA((14,)),
             pltpu.SemaphoreType.DMA((3, SAMPLES)),
             pltpu.SemaphoreType.DMA((3, SAMPLES)),
             pltpu.SemaphoreType.DMA((2, PEERS)),
             pltpu.SemaphoreType.DMA((2, PEERS)),
         ],
         compiler_params=pltpu.CompilerParams(
-            collective_id=0, has_side_effects=True, vmem_limit_bytes=50 * 2**20
+            collective_id=0, has_side_effects=True, vmem_limit_bytes=62 * 2**20
         ),
         cost_estimate=pl.CostEstimate(
             flops=10 * tokens * tokens * HEAD_DIM,
@@ -387,11 +421,40 @@
     )(cond, weight, hidden, incoming, q, k, v, g)
 
 
+def deliver_kernel(*refs):
+    count = (len(refs) - 2) // 3
+    sources, results, passing = refs[:count], refs[count : 2 * count], refs[2 * count : 3 * count]
+    arrived, done = refs[3 * count :]
+    loads = [pltpu.make_async_copy(sources[n], passing[n], arrived.at[n]) for n in range(count)]
+    stores = [pltpu.make_async_copy(passing[n], results[n], done.at[n]) for n in range(count)]
+    for load in loads:
+        load.start()
+    for load, store in zip(loads, stores):
+        load.wait()
+        store.start()
+    for store in stores:
+        store.wait()
+
+
+def deliver(results):
+    anywhere = pl.BlockSpec(memory_space=pl.ANY)
+    return pl.pallas_call(
+        deliver_kernel,
+        out_shape=[jax.ShapeDtypeStruct(r.shape, r.dtype) for r in results],
+        in_specs=[anywhere] * len(results),
+        out_specs=[anywhere] * len(results),
+        scratch_shapes=[pltpu.VMEM(r.shape, r.dtype) for r in results]
+        + [pltpu.SemaphoreType.DMA((len(results),))] * 2,
+        compiler_params=pltpu.CompilerParams(vmem_limit_bytes=62 * 2**20),
+    )(*results)
+
+
 def per_device(cond_vec, mod_weight, text_hidden, text_grad, queries, keys, values, out_grad):
     grads = joint(
         cond_vec, mod_weight, text_hidden[0], text_grad[0],
         queries[0], keys[0], values[0], out_grad[0],
     )
+    grads = deliver(grads)
     hidden_grad, weight_grad, cond_grad, query_grad, key_grad, value_grad = grads
     return (
         hidden_grad[None], weight_grad, cond_grad,

time: 129 us -> 117 us (0.907)
  local copies, waits for them, and re-layouts: 10.8 us -> 0 us
    unnamed x20 -> x0, local copies, waits for them, and re-layouts: 10.8 us -> none
    pallas_call x1, Pallas kernels: 117 us -> 114 us  [joint(): pl.pallas_call(joint_kernel, out_shape=[jax.ShapeDtypeStruct(hidden.shape...]
    pallas_call x0 -> x1, Pallas kernels: none -> 2.49 us  [deliver(): pl.pallas_call(deliver_kernel, out_shape=[jax.ShapeDtypeStruct(r.shape, r...]
where the time goes in v3:
time: 117 us
  Pallas kernels  116 us (99%)
    pallas_call x1, Pallas kernels, joint(): pl.pallas_call(joint_kernel, out_shape=[jax.ShapeDtypeStruct(hidden.shape...  114 us
    pallas_call x1, Pallas kernels, deliver(): pl.pallas_call(deliver_kernel, out_shape=[jax.ShapeDtypeStruct(r.shape, r...  2.49 us

profile of v3, /device:TPU:1, one launch (start us, length us, event | category | flops | bytes accessed | tf_op | source)
XLA Modules:
  0.0 117.0 jit_solution(11404449393286844938)
XLA Ops:
  0.6 113.9 %shard_map.127 = (bf16[32,3072]{1,0:T(8,128)(2,1)}, f32[2,192,96]{2,1,0:T(8,128)}, f32[1,192]{1,0:T(1,128)}, bf16[128,2048]{1,0:T(8,128)(2,1)}, bf16[128,2048]{1,0:T(8,128)(2,1)}, /*index=5*/bf16[128,2048]{1,0:T(8,128)(2,1)}) custom-call(f32[1,192]{1,0:T(1,128)} %cond_in.1, bf16[2,192,96]{2,1,0:T(8,128)(2,1)} %weight_in.1, bf16[32,3072]{1,0:T(8,128)(2,1)} %bitcast.17, ...), custom_call_target="tpu_custom_call" | custom-call | flops 5368709120 | bytes 3670016 | tf_op jit(solution)/shard_map/pallas_call | solution.py:371
  114.5 2.5 %shard_map.128 = (bf16[32,3072]{1,0:T(8,128)(2,1)}, f32[2,192,96]{2,1,0:T(8,128)}, f32[1,192]{1,0:T(1,128)}, bf16[128,2048]{1,0:T(8,128)(2,1)}, bf16[128,2048]{1,0:T(8,128)(2,1)}, /*index=5*/bf16[128,2048]{1,0:T(8,128)(2,1)}) custom-call(bf16[32,3072]{1,0:T(8,128)(2,1)} %get-tuple-element.18.refs_0_, f32[2,192,96]{2,1,0:T(8,128)} %get-tuple-element.19.refs_1_, ...), custom_call_target="tpu_custom_call" | custom-call | tf_op jit(solution)/shard_map/pallas_call | solution.py:441

commit v4 on v3

--- a/solution.py
+++ b/solution.py
@@ -13,6 +13,7 @@
 PEERS = 16
 SAMPLES = 32
 LANES = 128
+HIGH, LOW = 4, 8
 BLOCK = 4
 CHUNK = 256
 LOG2E = math.log2(math.e)
@@ -25,6 +26,14 @@
 
 def place_from(me, s):
     return ((me // 4 + 4 - s % 4) % 4) * 4 + (me % 4 + 4 - s // 4) % 4
+
+
+def rank_of(device):
+    return device % LOW * HIGH + device // LOW
+
+
+def device_of(rank):
+    return rank % HIGH * LOW + rank // HIGH
 
 
 def nt(a, b):
@@ -40,8 +49,10 @@
     hidden_grad_out, weight_grad_out, cond_grad_out, dq_ref, dk_ref, dv_ref,
     cond_ref, weight_ref, hidden_ref, incoming_ref, hidden_grad_ref, weight_grad_ref, cond_grad_ref,
     qb, kb, vb, gb, kt, u, dp, dka, dva, dqo, dko, dvo,
-    cond_own, cond_all, parcel, parcels, partial, share, whole, back, backs, row, normed, spread,
-    send, recv, local, dp_send, dp_recv, seq_send, seq_recv,
+    cond_own, cond_all, parcel, parcels, partial, share, whole, back, halves, half, backs,
+    row, normed, spread,
+    send, recv, local, dp_send, dp_recv, low_send, low_recv, high_send, high_recv,
+    seq_send, seq_recv,
 ):
     rows = q_ref.shape[0]
     width = qb.shape[2]
@@ -51,6 +62,7 @@
     factor = width ** (-0.5)
     me = lax.axis_index("seq")
     mine = lax.axis_index("dp")
+    low, high = mine % LOW, mine // LOW
     weight_rows, columns = weight_ref.shape[1:]
     features = hidden_ref.shape[1]
     text_rows = hidden_ref.shape[0]
@@ -98,13 +110,32 @@
     def other(r):
         return (mine + r) % SAMPLES
 
-    def dp_copy(step, r, arriving):
-        src = (cond_own, parcel.at[other(r)], back.at[other(r)])[step]
-        dst = (cond_all, parcels, backs)[step]
-        place = other(r) if arriving else mine
-        return pltpu.make_async_remote_copy(
-            src, dst.at[place], dp_send.at[step, r], dp_recv.at[step, place],
+    def dp_copy(r, arriving):
+        there = rank_of(other(r))
+        place = there if arriving else rank_of(mine)
+        return pltpu.make_async_remote_copy(
+            parcel.at[there], parcels.at[place], dp_send.at[r], dp_recv.at[place],
             device_id={"dp": other(r)}, device_id_type=MESH,
+        )
+
+    def high_copy(step, h, arriving):
+        there = (high + h) % HIGH
+        place = there if arriving else high
+        src = (cond_own, half.at[there])[step]
+        dst = (cond_all.at[low, place], backs.at[place])[step]
+        return pltpu.make_async_remote_copy(
+            src, dst, high_send.at[step, h], high_recv.at[step, place],
+            device_id={"dp": there * LOW + low}, device_id_type=MESH,
+        )
+
+    def low_copy(step, r, arriving):
+        there = (low + r) % LOW
+        place = there if arriving else low
+        src = (cond_all.at[low], back.at[there])[step]
+        dst = (cond_all.at[place], halves.at[place])[step]
+        return pltpu.make_async_remote_copy(
+            src, dst, low_send.at[step, r], low_recv.at[step, place],
+            device_id={"dp": high * LOW + there}, device_id_type=MESH,
         )
 
     def scatter_copy(s):
@@ -146,8 +177,12 @@
     cond_own[:, :weight_rows] = cond_ref[...]
     pl.semaphore_wait(barrier, PEERS + SAMPLES - 2)
 
-    each(1, SAMPLES, lambda r: dp_copy(0, r, False).start())
+    each(1, HIGH, lambda h: high_copy(0, h, False).start())
     each(1, PEERS, lambda s: inward(0, s).start())
+    cond_all[low, high] = cond_own[...]
+
+    each(1, HIGH, lambda h: high_copy(0, h, True).wait_recv())
+    each(1, LOW, lambda r: low_copy(0, r, False).start())
 
     fetch(1).wait()
     fetch(2).wait()
@@ -170,17 +205,17 @@
     parcel[...] = jnp.zeros_like(parcel)
     back[...] = jnp.zeros_like(back)
     for p in range(SAMPLES):
-        at = slice(p * columns, (p + 1) * columns)
+        first = device_of(p) * columns
+        at = slice(first, first + columns)
         parcel[p, :, LANES : LANES + columns] = plain[:, at]
         parcel[p, :, 2 * LANES : 2 * LANES + columns] = scaled[:, at]
 
-    cond_all[mine] = cond_own[...]
-    each(1, SAMPLES, lambda r: dp_copy(0, r, True).wait_recv())
-    cond = cond_all[...].reshape(SAMPLES, cond_all.shape[2])[:, :weight_rows]
+    each(1, LOW, lambda r: low_copy(0, r, True).wait_recv())
+    cond = cond_all[...].reshape(SAMPLES, cond_all.shape[3])[:, :weight_rows]
     act = (cond * jax.nn.sigmoid(cond)).astype(jnp.bfloat16)
     fetch(3).wait()
     parcel[:, :, :columns] = nn(act, weight_ref[1]).reshape(SAMPLES, 1, columns)
-    each(1, SAMPLES, lambda r: dp_copy(1, r, False).start())
+    each(1, SAMPLES, lambda r: dp_copy(r, False).start())
     each(1, PEERS, lambda s: inward(1, s).start())
 
     def send_block(i):
@@ -189,8 +224,8 @@
             inward(3, s).start()
 
     def scatter_sums():
-        parcels[mine] = parcel[mine]
-        each(1, SAMPLES, lambda r: dp_copy(1, r, True).wait_recv())
+        parcels[rank_of(mine)] = parcel[rank_of(mine)]
+        each(1, SAMPLES, lambda r: dp_copy(r, True).wait_recv())
         each(1, PEERS, lambda s: scatter_copy(s).start())
 
     def gather_sums():
@@ -203,7 +238,7 @@
         whole[pl.ds(me * 2, 2)] = share[...]
         each(1, PEERS, lambda s: gather_copy(s, True).wait_recv())
         sums = whole[...].reshape(SAMPLES, whole.shape[2])
-        cond = cond_all[...].reshape(SAMPLES, cond_all.shape[2])[:, :weight_rows]
+        cond = cond_all[...].reshape(SAMPLES, cond_all.shape[3])[:, :weight_rows]
         act = (cond * jax.nn.sigmoid(cond)).astype(jnp.bfloat16).astype(jnp.float32)
         backward = jnp.zeros((SAMPLES, weight_rows), jnp.float32)
         for k in range(2):
@@ -217,12 +252,19 @@
                 precision=lax.Precision.HIGHEST, preferred_element_type=jnp.float32,
             )
         keep(0).start()
-        back[:, :, :weight_rows] = backward.reshape(SAMPLES, 1, weight_rows)
-        each(1, SAMPLES, lambda r: dp_copy(2, r, False).start())
+        back[:, :, :, :weight_rows] = backward.reshape(LOW, HIGH, 1, weight_rows)
+        each(1, LOW, lambda r: low_copy(1, r, False).start())
+
+    def half_sums():
+        halves[low] = back[low]
+        each(1, LOW, lambda r: low_copy(1, r, True).wait_recv())
+        half[...] = jnp.sum(halves[...], axis=0)
+        each(1, HIGH, lambda h: high_copy(1, h, False).start())
 
     def text_gradient():
         for j in range(SAMPLES):
-            row[:, j * columns : (j + 1) * columns] = whole[j, :, :columns]
+            first = device_of(j) * columns
+            row[:, first : first + columns] = whole[j, :, :columns]
         gain = 1.0 + row[...]
         for t in range(0, text_rows, 16):
             at = slice(t, t + 16)
@@ -235,8 +277,8 @@
         keep(1).start()
 
     def cond_gradient():
-        backs[mine] = back[mine]
-        each(1, SAMPLES, lambda r: dp_copy(2, r, True).wait_recv())
+        backs[high] = half[high]
+        each(1, HIGH, lambda h: high_copy(1, h, True).wait_recv())
         summed = jnp.sum(backs[...], axis=0)[:, :weight_rows]
         cond = cond_ref[...]
         sigma = jax.nn.sigmoid(cond)
@@ -316,6 +358,8 @@
             weight_gradients()
             send_block(3)
 
+        pl.when(i == 1)(half_sums)
+
     own_out(0).start()
     for s in range(PEERS):
         at = slice(s * rows, (s + 1) * rows)
@@ -334,8 +378,11 @@
 
     @pl.loop(1, SAMPLES)
     def _(r):
-        for step in range(3):
-            dp_copy(step, r, False).wait_send()
+        dp_copy(r, False).wait_send()
+
+    for step in range(2):
+        each(1, HIGH, lambda h: high_copy(step, h, False).wait_send())
+        each(1, LOW, lambda r: low_copy(step, r, False).wait_send())
 
     @pl.loop(1, PEERS)
     def _(s):
@@ -391,22 +438,28 @@
             scores, scores, total, total,
             slots, slots, slots,
             pltpu.VMEM((1, padded), f32),
-            pltpu.VMEM((SAMPLES, 1, padded), f32),
+            pltpu.VMEM((LOW, HIGH, 1, padded), f32),
             pltpu.VMEM((SAMPLES, 1, 3 * LANES), f32),
             pltpu.VMEM((SAMPLES, 1, 3 * LANES), f32),
             pltpu.VMEM((PEERS, 2, 1, 3 * LANES), f32),
             pltpu.VMEM((2, 1, 3 * LANES), f32),
             pltpu.VMEM((SAMPLES, 1, 3 * LANES), f32),
-            pltpu.VMEM((SAMPLES, 1, padded), f32),
-            pltpu.VMEM((SAMPLES, 1, padded), f32),
+            pltpu.VMEM((LOW, HIGH, 1, padded), f32),
+            pltpu.VMEM((LOW, HIGH, 1, padded), f32),
+            pltpu.VMEM((HIGH, 1, padded), f32),
+            pltpu.VMEM((HIGH, 1, padded), f32),
             pltpu.VMEM((1, hidden.shape[1]), f32),
             pltpu.VMEM(hidden.shape, f32),
             pltpu.VMEM((hidden.shape[0], LANES), f32),
             pltpu.SemaphoreType.DMA((7, PEERS)),
             pltpu.SemaphoreType.DMA((7, PEERS)),
             pltpu.SemaphoreType.DMA((14,)),
-            pltpu.SemaphoreType.DMA((3, SAMPLES)),
-            pltpu.SemaphoreType.DMA((3, SAMPLES)),
+            pltpu.SemaphoreType.DMA((SAMPLES,)),
+            pltpu.SemaphoreType.DMA((SAMPLES,)),
+            pltpu.SemaphoreType.DMA((2, LOW)),
+            pltpu.SemaphoreType.DMA((2, LOW)),
+            pltpu.SemaphoreType.DMA((2, HIGH)),
+            pltpu.SemaphoreType.DMA((2, HIGH)),
             pltpu.SemaphoreType.DMA((2, PEERS)),
             pltpu.SemaphoreType.DMA((2, PEERS)),
         ],

time: 117 us -> 113 us (0.966); the launches traced: 117 us -> 111 us
  Pallas kernels: 116 us -> 111 us
    pallas_call x1, Pallas kernels: 114 us -> 108 us  [joint(): pl.pallas_call(joint_kernel, out_shape=[jax.ShapeDtypeStruct(hidden.shape...]
where the time goes in v4:
time: 113 us; the launch traced here: 111 us
  Pallas kernels  111 us (98%)
    pallas_call x1, Pallas kernels, joint(): pl.pallas_call(joint_kernel, out_shape=[jax.ShapeDtypeStruct(hidden.shape...  108 us
    pallas_call x1, Pallas kernels, deliver(): pl.pallas_call(deliver_kernel, out_shape=[jax.ShapeDtypeStruct(r.shape, r...  2.49 us

profile of v4, /device:TPU:1, one launch (start us, length us, event | category | flops | bytes accessed | tf_op | source)
XLA Modules:
  0.0 111.2 jit_solution(11192288245848212094)
XLA Ops:
  0.6 108.0 %shard_map.127 = (bf16[32,3072]{1,0:T(8,128)(2,1)}, f32[2,192,96]{2,1,0:T(8,128)}, f32[1,192]{1,0:T(1,128)}, bf16[128,2048]{1,0:T(8,128)(2,1)}, bf16[128,2048]{1,0:T(8,128)(2,1)}, /*index=5*/bf16[128,2048]{1,0:T(8,128)(2,1)}) custom-call(f32[1,192]{1,0:T(1,128)} %cond_in.1, bf16[2,192,96]{2,1,0:T(8,128)(2,1)} %weight_in.1, bf16[32,3072]{1,0:T(8,128)(2,1)} %bitcast.17, ...), custom_call_target="tpu_custom_call" | custom-call | flops 5368709120 | bytes 3670016 | tf_op jit(solution)/shard_map/pallas_call | solution.py:418
  108.7 2.5 %shard_map.128 = (bf16[32,3072]{1,0:T(8,128)(2,1)}, f32[2,192,96]{2,1,0:T(8,128)}, f32[1,192]{1,0:T(1,128)}, bf16[128,2048]{1,0:T(8,128)(2,1)}, bf16[128,2048]{1,0:T(8,128)(2,1)}, /*index=5*/bf16[128,2048]{1,0:T(8,128)(2,1)}) custom-call(bf16[32,3072]{1,0:T(8,128)(2,1)} %get-tuple-element.18.refs_0_, f32[2,192,96]{2,1,0:T(8,128)} %get-tuple-element.19.refs_1_, ...), custom_call_target="tpu_custom_call" | custom-call | tf_op jit(solution)/shard_map/pallas_call | solution.py:494

commit v5 on v4

--- a/solution.py
+++ b/solution.py
@@ -52,7 +52,7 @@
     cond_own, cond_all, parcel, parcels, partial, share, whole, back, halves, half, backs,
     row, normed, spread,
     send, recv, local, dp_send, dp_recv, low_send, low_recv, high_send, high_recv,
-    seq_send, seq_recv,
+    seq_send, seq_recv, entered, opened,
 ):
     rows = q_ref.shape[0]
     width = qb.shape[2]
@@ -162,27 +162,59 @@
 
     barrier = pltpu.get_barrier_semaphore()
 
-    @pl.loop(1, SAMPLES)
+    def signal(semaphore, **device):
+        pl.semaphore_signal(semaphore, inc=1, device_id=device, device_id_type=MESH)
+
+    def is_gateway(low, seq):
+        return low == seq % LOW
+
+    gateway = is_gateway(low, me)
+    member = jnp.logical_not(gateway)
+
+    @pl.loop(1, LOW)
     def _(r):
-        pl.semaphore_signal(barrier, inc=1, device_id={"dp": other(r)}, device_id_type=MESH)
+        there = (low + r) % LOW
+
+        @pl.when(jnp.logical_not(is_gateway(there, me)))
+        def _():
+            signal(barrier, dp=high * LOW + there)
 
     @pl.loop(1, PEERS)
     def _(s):
-        pl.semaphore_signal(
-            barrier, inc=1, device_id={"seq": place_to(me, s)}, device_id_type=MESH
-        )
+        there = place_to(me, s)
+
+        @pl.when(jnp.logical_not(is_gateway(low, there)))
+        def _():
+            signal(barrier, seq=there)
 
     cond_own[...] = jnp.zeros_like(cond_own)
     fetch(0).wait()
     cond_own[:, :weight_rows] = cond_ref[...]
-    pl.semaphore_wait(barrier, PEERS + SAMPLES - 2)
-
-    each(1, HIGH, lambda h: high_copy(0, h, False).start())
+
+    @pl.when(member)
+    def _():
+        pl.semaphore_wait(barrier, PEERS + LOW - 2)
+        for there in range(0, PEERS, LOW):
+            signal(entered, seq=low + there)
+        signal(entered, dp=high * LOW + me % LOW)
+
+    @pl.when(gateway)
+    def _():
+        pl.semaphore_wait(entered, PEERS - PEERS // LOW + LOW - 1)
+        for h in range(1, HIGH):
+            signal(barrier, dp=(high + h) % HIGH * LOW + low)
+
+
     each(1, PEERS, lambda s: inward(0, s).start())
+    each(1, PEERS, lambda s: inward(1, s).start())
+
+    def send_block(i):
+        for s in range(max(i * BLOCK, 1), (i + 1) * BLOCK):
+            inward(2, s).start()
+            inward(3, s).start()
+
+    send_block(0)
     cond_all[low, high] = cond_own[...]
-
-    each(1, HIGH, lambda h: high_copy(0, h, True).wait_recv())
-    each(1, LOW, lambda r: low_copy(0, r, False).start())
 
     fetch(1).wait()
     fetch(2).wait()
@@ -210,18 +242,25 @@
         parcel[p, :, LANES : LANES + columns] = plain[:, at]
         parcel[p, :, 2 * LANES : 2 * LANES + columns] = scaled[:, at]
 
+    @pl.when(gateway)
+    def _():
+        pl.semaphore_wait(barrier, HIGH - 1)
+        for r in range(1, LOW):
+            signal(opened, dp=high * LOW + (low + r) % LOW)
+
+    @pl.when(member)
+    def _():
+        pl.semaphore_wait(opened, 1)
+
+    each(1, HIGH, lambda h: high_copy(0, h, False).start())
+    each(1, HIGH, lambda h: high_copy(0, h, True).wait_recv())
+    each(1, LOW, lambda r: low_copy(0, r, False).start())
     each(1, LOW, lambda r: low_copy(0, r, True).wait_recv())
     cond = cond_all[...].reshape(SAMPLES, cond_all.shape[3])[:, :weight_rows]
     act = (cond * jax.nn.sigmoid(cond)).astype(jnp.bfloat16)
     fetch(3).wait()
     parcel[:, :, :columns] = nn(act, weight_ref[1]).reshape(SAMPLES, 1, columns)
     each(1, SAMPLES, lambda r: dp_copy(r, False).start())
-    each(1, PEERS, lambda s: inward(1, s).start())
-
-    def send_block(i):
-        for s in range(max(i * BLOCK, 1), (i + 1) * BLOCK):
-            inward(2, s).start()
-            inward(3, s).start()
 
     def scatter_sums():
         parcels[rank_of(mine)] = parcel[rank_of(mine)]
@@ -294,12 +333,10 @@
     for s in range(PEERS):
         kt[:, s * rows : (s + 1) * rows] = kb[s].astype(jnp.float32).T.astype(jnp.bfloat16)
 
+    send_block(1)
+    each(1, PEERS, lambda s: inward(1, s).wait_recv())
+    send_block(2)
     scatter_sums()
-    send_block(0)
-    each(1, PEERS, lambda s: inward(1, s).wait_recv())
-    gather_sums()
-    send_block(1)
-    send_block(2)
 
     per_chunk = CHUNK // rows
 
@@ -355,10 +392,11 @@
 
         @pl.when(i == 0)
         def _():
-            weight_gradients()
             send_block(3)
-
-        pl.when(i == 1)(half_sums)
+            gather_sums()
+
+        pl.when(i == 1)(weight_gradients)
+        pl.when(i == 2)(half_sums)
 
     own_out(0).start()
     for s in range(PEERS):
@@ -462,6 +500,8 @@
             pltpu.SemaphoreType.DMA((2, HIGH)),
             pltpu.SemaphoreType.DMA((2, PEERS)),
             pltpu.SemaphoreType.DMA((2, PEERS)),
+            pltpu.SemaphoreType.REGULAR,
+            pltpu.SemaphoreType.REGULAR,
         ],
         compiler_params=pltpu.CompilerParams(
             collective_id=0, has_side_effects=True, vmem_limit_bytes=62 * 2**20

time: 113 us -> 121 us (1.071); the launches traced: 111 us -> 121 us
  Pallas kernels: 111 us -> 120 us
    pallas_call x1, Pallas kernels: 108 us -> 118 us  [joint(): pl.pallas_call(joint_kernel, out_shape=[jax.ShapeDtypeStruct(hidden.shape...]
where the time goes in v5:
time: 121 us
  Pallas kernels  120 us (99%)
    pallas_call x1, Pallas kernels, joint(): pl.pallas_call(joint_kernel, out_shape=[jax.ShapeDtypeStruct(hidden.shape...  118 us
    pallas_call x1, Pallas kernels, deliver(): pl.pallas_call(deliver_kernel, out_shape=[jax.ShapeDtypeStruct(r.shape, r...  2.49 us

profile of v5, /device:TPU:1, one launch (start us, length us, event | category | flops | bytes accessed | tf_op | source)
XLA Modules:
  0.0 120.7 jit_solution(5395745895710293853)
XLA Ops:
  0.6 117.5 %shard_map.127 = (bf16[32,3072]{1,0:T(8,128)(2,1)}, f32[2,192,96]{2,1,0:T(8,128)}, f32[1,192]{1,0:T(1,128)}, bf16[128,2048]{1,0:T(8,128)(2,1)}, bf16[128,2048]{1,0:T(8,128)(2,1)}, /*index=5*/bf16[128,2048]{1,0:T(8,128)(2,1)}) custom-call(f32[1,192]{1,0:T(1,128)} %cond_in.1, bf16[2,192,96]{2,1,0:T(8,128)(2,1)} %weight_in.1, bf16[32,3072]{1,0:T(8,128)(2,1)} %bitcast.17, ...), custom_call_target="tpu_custom_call" | custom-call | flops 5368709120 | bytes 3670016 | tf_op jit(solution)/shard_map/pallas_call | solution.py:456
  118.2 2.5 %shard_map.128 = (bf16[32,3072]{1,0:T(8,128)(2,1)}, f32[2,192,96]{2,1,0:T(8,128)}, f32[1,192]{1,0:T(1,128)}, bf16[128,2048]{1,0:T(8,128)(2,1)}, bf16[128,2048]{1,0:T(8,128)(2,1)}, /*index=5*/bf16[128,2048]{1,0:T(8,128)(2,1)}) custom-call(bf16[32,3072]{1,0:T(8,128)(2,1)} %get-tuple-element.18.refs_0_, f32[2,192,96]{2,1,0:T(8,128)} %get-tuple-element.19.refs_1_, ...), custom_call_target="tpu_custom_call" | custom-call | tf_op jit(solution)/shard_map/pallas_call | solution.py:534

commit v6 on v5

--- a/solution.py
+++ b/solution.py
@@ -206,14 +206,12 @@
 
 
     each(1, PEERS, lambda s: inward(0, s).start())
-    each(1, PEERS, lambda s: inward(1, s).start())
 
     def send_block(i):
         for s in range(max(i * BLOCK, 1), (i + 1) * BLOCK):
             inward(2, s).start()
             inward(3, s).start()
 
-    send_block(0)
     cond_all[low, high] = cond_own[...]
 
     fetch(1).wait()
@@ -253,14 +251,18 @@
         pl.semaphore_wait(opened, 1)
 
     each(1, HIGH, lambda h: high_copy(0, h, False).start())
+    each(1, PEERS, lambda s: inward(1, s).start())
+    send_block(0)
     each(1, HIGH, lambda h: high_copy(0, h, True).wait_recv())
     each(1, LOW, lambda r: low_copy(0, r, False).start())
+    send_block(1)
     each(1, LOW, lambda r: low_copy(0, r, True).wait_recv())
     cond = cond_all[...].reshape(SAMPLES, cond_all.shape[3])[:, :weight_rows]
     act = (cond * jax.nn.sigmoid(cond)).astype(jnp.bfloat16)
     fetch(3).wait()
     parcel[:, :, :columns] = nn(act, weight_ref[1]).reshape(SAMPLES, 1, columns)
     each(1, SAMPLES, lambda r: dp_copy(r, False).start())
+    send_block(2)
 
     def scatter_sums():
         parcels[rank_of(mine)] = parcel[rank_of(mine)]
@@ -333,10 +335,7 @@
     for s in range(PEERS):
         kt[:, s * rows : (s + 1) * rows] = kb[s].astype(jnp.float32).T.astype(jnp.bfloat16)
 
-    send_block(1)
     each(1, PEERS, lambda s: inward(1, s).wait_recv())
-    send_block(2)
-    scatter_sums()
 
     per_chunk = CHUNK // rows
 
@@ -393,23 +392,22 @@
         @pl.when(i == 0)
         def _():
             send_block(3)
-            gather_sums()
-
-        pl.when(i == 1)(weight_gradients)
-        pl.when(i == 2)(half_sums)
+
+        pl.when(i == 1)(scatter_sums)
+        pl.when(i == 2)(gather_sums)
+        pl.when(i == 3)(weight_gradients)
 
     own_out(0).start()
     for s in range(PEERS):
         at = slice(s * rows, (s + 1) * rows)
         dko[s] = (dka[at] * factor).astype(jnp.bfloat16)
+    each(1, PEERS, lambda s: outward(1, s).start())
+    own_out(1).start()
+    half_sums()
+    for s in range(PEERS):
+        at = slice(s * rows, (s + 1) * rows)
         dvo[s] = dva[at].astype(jnp.bfloat16)
-
-    @pl.loop(1, PEERS)
-    def _(s):
-        outward(1, s).start()
-        outward(2, s).start()
-
-    own_out(1).start()
+    each(1, PEERS, lambda s: outward(2, s).start())
     own_out(2).start()
     text_gradient()
     cond_gradient()

time: 121 us -> 113 us (0.934)
  Pallas kernels: 120 us -> 112 us
    pallas_call x1, Pallas kernels: 118 us -> 109 us  [joint(): pl.pallas_call(joint_kernel, out_shape=[jax.ShapeDtypeStruct(hidden.shape...]
where the time goes in v6:
time: 113 us; the launch traced here: 112 us
  Pallas kernels  112 us (99%)
    pallas_call x1, Pallas kernels, joint(): pl.pallas_call(joint_kernel, out_shape=[jax.ShapeDtypeStruct(hidden.shape...  109 us
    pallas_call x1, Pallas kernels, deliver(): pl.pallas_call(deliver_kernel, out_shape=[jax.ShapeDtypeStruct(r.shape, r...  2.49 us

profile of v6, /device:TPU:1, one launch (start us, length us, event | category | flops | bytes accessed | tf_op | source)
XLA Modules:
  0.0 112.4 jit_solution(17584928450655828385)
XLA Ops:
  0.6 109.3 %shard_map.127 = (bf16[32,3072]{1,0:T(8,128)(2,1)}, f32[2,192,96]{2,1,0:T(8,128)}, f32[1,192]{1,0:T(1,128)}, bf16[128,2048]{1,0:T(8,128)(2,1)}, bf16[128,2048]{1,0:T(8,128)(2,1)}, /*index=5*/bf16[128,2048]{1,0:T(8,128)(2,1)}) custom-call(f32[1,192]{1,0:T(1,128)} %cond_in.1, bf16[2,192,96]{2,1,0:T(8,128)(2,1)} %weight_in.1, bf16[32,3072]{1,0:T(8,128)(2,1)} %bitcast.17, ...), custom_call_target="tpu_custom_call" | custom-call | flops 5368709120 | bytes 3670016 | tf_op jit(solution)/shard_map/pallas_call | solution.py:454
  109.9 2.5 %shard_map.128 = (bf16[32,3072]{1,0:T(8,128)(2,1)}, f32[2,192,96]{2,1,0:T(8,128)}, f32[1,192]{1,0:T(1,128)}, bf16[128,2048]{1,0:T(8,128)(2,1)}, bf16[128,2048]{1,0:T(8,128)(2,1)}, /*index=5*/bf16[128,2048]{1,0:T(8,128)(2,1)}) custom-call(bf16[32,3072]{1,0:T(8,128)(2,1)} %get-tuple-element.18.refs_0_, f32[2,192,96]{2,1,0:T(8,128)} %get-tuple-element.19.refs_1_, ...), custom_call_target="tpu_custom_call" | custom-call | tf_op jit(solution)/shard_map/pallas_call | solution.py:532
